TPU v7x, 32 devices: a whole 2x2x4 slice. The times are simulated.
32 devices in a mesh: seq: 4 (over z), roll: 2 (over x), head: 4 (over y, core).
Axes of the slice: x: 2, y: 2, z: 4, core: 2. Of those that a mesh axis runs over, the one named last changes fastest.
Arguments:
- queries: bfloat16 [2, 768, 64, 128], P('roll', 'seq', 'head'), may hold values from -7 to 7
- rollout_keys: bfloat16 [2, 768, 8, 128], P('roll', 'seq', 'head'), may hold values from -6 to 6
- rollout_values: bfloat16 [2, 768, 8, 128], P('roll', 'seq', 'head'), may hold values from -24 to 24
- prompt_keys: bfloat16 [1024, 8, 128], P(('seq', 'roll'), 'head'), may hold values from -4.5 to 4.5
- prompt_values: bfloat16 [1024, 8, 128], P(('seq', 'roll'), 'head'), may hold values from -24 to 24
- grad_out: bfloat16 [2, 768, 64, 128], P('roll', 'seq', 'head'), may hold values from -24 to 24
- lengths: int32 [2], P('roll'), may hold values from 192 to 768, as said below
Outputs:
- attention_out: bfloat16 [2, 768, 64, 128], P('roll', 'seq', 'head')
- grad_queries: bfloat16 [2, 768, 64, 128], P('roll', 'seq', 'head')
- grad_rollout_keys: bfloat16 [2, 768, 8, 128], P('roll', 'seq', 'head')
- grad_rollout_values: bfloat16 [2, 768, 8, 128], P('roll', 'seq', 'head')
- grad_prompt_keys: bfloat16 [1024, 8, 128], P(('seq', 'roll'), 'head')
- grad_prompt_values: bfloat16 [1024, 8, 128], P(('seq', 'roll'), 'head')
Inputs may be any that keep to these rules, and one draw needn't show every extreme that they name: `lengths`: every rollout's length is at least 192, and one rollout of each draw has all 768 positions live.
All inputs are finite; a program needn't handle non-finite values.
Results may differ from a plain program's by a relative error of at most 0.007.
Values may be sent and summed in bfloat16 or wider, within the bound.
No kernel may reach another device: no remote copies, remote signals or barrier semaphores. Data moves between devices by JAX's collectives and lax.ppermute only.
A program may use at most 128 MiB of HBM per device.

v0:
```python
import math

import jax
import jax.numpy as jnp
from jax import lax
from jax.sharding import PartitionSpec as P


def scores_for(query_grid, key_block, key_pos, query_pos, score_scale):
    scores = (
        jnp.einsum("ngqd,kgd->gqnk", query_grid, key_block, preferred_element_type=jnp.float32)
        * score_scale
    )
    allowed = key_pos[None, :] <= query_pos[:, None]
    return jnp.where(allowed[None, None], scores, -jnp.inf)


def max_block(maxima, query_grid, key_block, key_pos, query_pos, score_scale):
    scores = scores_for(query_grid, key_block, key_pos, query_pos, score_scale)
    return jnp.maximum(maxima, jnp.max(scores, -1))


def forward_block(
    running, maxima, query_grid, key_block, value_block, key_pos, query_pos, score_scale
):
    totals, summed = running
    scores = scores_for(query_grid, key_block, key_pos, query_pos, score_scale)
    lifted = jnp.exp(scores - maxima[..., None])
    totals = totals + jnp.sum(lifted, -1)
    summed = summed + jnp.einsum(
        "gqnk,kgd->gqnd",
        lifted.astype(jnp.bfloat16),
        value_block,
        preferred_element_type=jnp.float32,
    )
    return (totals, summed)


def score_grads(
    query_grid,
    cot_grid,
    key_block,
    value_block,
    key_pos,
    query_pos,
    log_total,
    offsets,
    score_scale,
):
    scores = scores_for(query_grid, key_block, key_pos, query_pos, score_scale)
    weights = jnp.exp(scores - log_total[..., None])
    grad_weights = jnp.einsum(
        "ngqd,kgd->gqnk", cot_grid, value_block, preferred_element_type=jnp.float32
    )
    grad_scores = (weights * (grad_weights - offsets[..., None]) * score_scale).astype(jnp.bfloat16)
    return (grad_scores, weights.astype(jnp.bfloat16))


def backward_block(
    query_grid,
    cot_grid,
    key_block,
    value_block,
    key_pos,
    query_pos,
    log_total,
    offsets,
    score_scale,
):
    grad_scores, weights_low = score_grads(
        query_grid,
        cot_grid,
        key_block,
        value_block,
        key_pos,
        query_pos,
        log_total,
        offsets,
        score_scale,
    )
    grad_query = jnp.einsum(
        "gqnk,kgd->ngqd", grad_scores, key_block, preferred_element_type=jnp.float32
    )
    grad_key = jnp.einsum(
        "gqnk,ngqd->kgd", grad_scores, query_grid, preferred_element_type=jnp.float32
    )
    grad_value = jnp.einsum(
        "gqnk,ngqd->kgd", weights_low, cot_grid, preferred_element_type=jnp.float32
    )
    return (grad_query, grad_key, grad_value)


def local(queries, rollout_keys, rollout_values, prompt_keys, prompt_values, grad_out, lengths):
    query_rows = queries[0]
    row_count, head_count, head_dim = query_rows.shape
    group_count = rollout_keys.shape[2]
    per_group = head_count // group_count
    query_grid = query_rows.reshape(row_count, group_count, per_group, head_dim)
    score_scale = head_dim ** (-0.5)
    first_row = lax.axis_index("seq") * row_count
    last_row = first_row + row_count - 1
    query_pos = first_row + jnp.arange(row_count, dtype=jnp.int32)
    seq_length = lengths[0]
    device_live = first_row < seq_length
    total_rows = row_count * lax.axis_size("seq")
    prompt_full_keys, prompt_full_values = (
        lax.all_gather(prompt_keys, ("seq", "roll"), axis=0, tiled=True),
        lax.all_gather(prompt_values, ("seq", "roll"), axis=0, tiled=True),
    )
    prompt_rows = prompt_full_keys.shape[0]
    span_rows = math.gcd(math.gcd(prompt_rows, total_rows), 512)
    prompt_pos = jnp.full((span_rows,), -1, jnp.int32)
    own_keys = rollout_keys[0]
    own_values = rollout_values[0]
    stat_shape = (group_count, per_group, row_count)
    maxima = jnp.full(stat_shape, -jnp.inf, jnp.float32)
    for counter in range(prompt_rows // span_rows):
        lower = counter * span_rows
        maxima = max_block(
            maxima,
            query_grid,
            prompt_full_keys[lower : lower + span_rows],
            prompt_pos,
            query_pos,
            score_scale,
        )

    def rollout_max(carried, key_block, block_start):
        key_pos = block_start + jnp.arange(key_block.shape[0], dtype=jnp.int32)
        return lax.cond(
            (block_start <= last_row) & device_live,
            lambda inner: max_block(inner, query_grid, key_block, key_pos, query_pos, score_scale),
            lambda inner: inner,
            carried,
        )

    gathered_keys, gathered_values = (
        lax.all_gather(own_keys, "seq", axis=0, tiled=True),
        lax.all_gather(own_values, "seq", axis=0, tiled=True),
    )

    def max_loop(counter, carried):
        block_start = counter * span_rows
        key_block = lax.dynamic_slice_in_dim(gathered_keys, block_start, span_rows, 0)
        return rollout_max(carried, key_block, block_start)

    maxima = lax.fori_loop(0, total_rows // span_rows, max_loop, maxima)
    running = (jnp.zeros(stat_shape, jnp.float32), jnp.zeros(stat_shape + (head_dim,), jnp.float32))
    for counter in range(prompt_rows // span_rows):
        lower = counter * span_rows
        running = forward_block(
            running,
            maxima,
            query_grid,
            prompt_full_keys[lower : lower + span_rows],
            prompt_full_values[lower : lower + span_rows],
            prompt_pos,
            query_pos,
            score_scale,
        )

    def forward_loop(counter, carried):
        block_start = counter * span_rows
        key_block = lax.dynamic_slice_in_dim(gathered_keys, block_start, span_rows, 0)
        value_block = lax.dynamic_slice_in_dim(gathered_values, block_start, span_rows, 0)
        key_pos = block_start + jnp.arange(span_rows, dtype=jnp.int32)
        return lax.cond(
            (block_start <= last_row) & device_live,
            lambda inner: forward_block(
                inner, maxima, query_grid, key_block, value_block, key_pos, query_pos, score_scale
            ),
            lambda inner: inner,
            carried,
        )

    running = lax.fori_loop(0, total_rows // span_rows, forward_loop, running)
    totals, summed = running
    normalized = summed / totals[..., None]
    row_valid = query_pos < seq_length
    flat_out = normalized.transpose(2, 0, 1, 3).reshape(row_count, head_count, head_dim)
    attention_rows = jnp.where(row_valid[:, None, None], flat_out, 0.0).astype(jnp.bfloat16)
    log_total = maxima + jnp.log(totals)
    cot_rows = jnp.where(row_valid[:, None, None], grad_out[0], jnp.zeros_like(grad_out[0]))
    cot_grid = cot_rows.reshape(row_count, group_count, per_group, head_dim)
    offsets = jnp.sum(cot_grid.transpose(1, 2, 0, 3).astype(jnp.float32) * normalized, -1)
    grad_query = jnp.zeros((row_count, group_count, per_group, head_dim), jnp.float32)
    prompt_key_parts = []
    prompt_value_parts = []
    for counter in range(prompt_rows // span_rows):
        lower = counter * span_rows
        block_grads = backward_block(
            query_grid,
            cot_grid,
            prompt_full_keys[lower : lower + span_rows],
            prompt_full_values[lower : lower + span_rows],
            prompt_pos,
            query_pos,
            log_total,
            offsets,
            score_scale,
        )
        grad_query = grad_query + block_grads[0]
        prompt_key_parts.append(block_grads[1])
        prompt_value_parts.append(block_grads[2])
    prompt_key_terms = jnp.concatenate(prompt_key_parts, axis=0)
    prompt_value_terms = jnp.concatenate(prompt_value_parts, axis=0)

    def backward_loop(counter, carried):
        block_start = counter * span_rows
        key_block = lax.dynamic_slice_in_dim(gathered_keys, block_start, span_rows, 0)
        value_block = lax.dynamic_slice_in_dim(gathered_values, block_start, span_rows, 0)
        key_pos = block_start + jnp.arange(span_rows, dtype=jnp.int32)

        def accumulate(carried_in):
            query_acc, key_acc, value_acc = carried_in
            block_grads = backward_block(
                query_grid,
                cot_grid,
                key_block,
                value_block,
                key_pos,
                query_pos,
                log_total,
                offsets,
                score_scale,
            )
            key_acc = lax.dynamic_update_slice_in_dim(key_acc, block_grads[1], block_start, 0)
            value_acc = lax.dynamic_update_slice_in_dim(value_acc, block_grads[2], block_start, 0)
            return (query_acc + block_grads[0], key_acc, value_acc)

        return lax.cond(
            (block_start <= last_row) & device_live,
            accumulate,
            lambda carried_in: carried_in,
            carried,
        )

    zero_keys = jnp.zeros((total_rows, group_count, head_dim), jnp.float32)
    grad_query, key_grads, value_grads = lax.fori_loop(
        0, total_rows // span_rows, backward_loop, (grad_query, zero_keys, zero_keys)
    )
    rollout_key_sum, rollout_value_sum = (
        lax.psum_scatter(key_grads, "seq", scatter_dimension=0, tiled=True),
        lax.psum_scatter(value_grads, "seq", scatter_dimension=0, tiled=True),
    )
    prompt_key_sum, prompt_value_sum = (
        lax.psum_scatter(prompt_key_terms, ("seq", "roll"), scatter_dimension=0, tiled=True),
        lax.psum_scatter(prompt_value_terms, ("seq", "roll"), scatter_dimension=0, tiled=True),
    )
    grad_rows = grad_query.reshape(row_count, head_count, head_dim).astype(jnp.bfloat16)
    return (
        attention_rows[None],
        grad_rows[None],
        rollout_key_sum.astype(jnp.bfloat16)[None],
        rollout_value_sum.astype(jnp.bfloat16)[None],
        prompt_key_sum.astype(jnp.bfloat16),
        prompt_value_sum.astype(jnp.bfloat16),
    )


def solution(mesh):
    placed = (
        P("roll", "seq", "head", None),
        P("roll", "seq", "head", None),
        P("roll", "seq", "head", None),
        P(("seq", "roll"), "head", None),
        P(("seq", "roll"), "head", None),
        P("roll", "seq", "head", None),
        P("roll"),
    )
    return jax.shard_map(
        local,
        mesh=mesh,
        in_specs=placed,
        out_specs=(
            P("roll", "seq", "head", None),
            P("roll", "seq", "head", None),
            P("roll", "seq", "head", None),
            P("roll", "seq", "head", None),
            P(("seq", "roll"), "head", None),
            P(("seq", "roll"), "head", None),
        ),
        check_vma=False,
    )
```

profile of v0, /device:TPU:0, one launch (start us, length us, event | category | flops | bytes accessed | tf_op | source)
XLA Modules:
  0.0 294.3 jit_solution(3158643620926642935)
XLA Ops:
  7.2 1.3 copy.34
  9.4 33.0 %all_gather.12 = bf16[1024,2,128]{2,0,1:T(8,128)(2,1)S(1)} all-gather(bf16[128,2,128]{2,0,1:T(8,128)(2,1)S(1)} %copy.33), channel_id=1, replica_groups=mesh['seq'=4,'roll'=2,'head'=4] {'seq','roll'}, dimensions={0}, use_global_device_ids=true | all-gather | bytes 589824 | tf_op jit(solution)/shard_map/all_gather | solution.py:107
  42.4 2.4 bitcast_reduce_fusion
  44.8 2.3 bitcast_reduce_fusion.1
  47.1 2.3 bitcast_reduce_fusion.3
  49.5 2.3 bitcast_reduce_fusion.2
  52.5 14.4 %all-gather = bf16[1,768,2,128]{3,1,2,0:T(8,128)(2,1)S(1)} all-gather(bf16[1,192,2,128]{3,1,2,0:T(8,128)(2,1)S(1)} %copy.35), channel_id=2, replica_groups=mesh['seq'=4,'roll'=2,'head'=4] {'seq'}, dimensions={1}, use_global_device_ids=true | all-gather | bytes 491520 | tf_op jit(solution)/shard_map/all_gather | solution.py:138
  66.9 1.2 while.51
  66.9 1.0 conditional.9
  68.2 33.3 %all_gather.14 = bf16[1024,2,128]{2,0,1:T(8,128)(2,1)S(1)} all-gather(bf16[128,2,128]{2,0,1:T(8,128)(2,1)S(1)} %copy.36), channel_id=1, replica_groups=mesh['seq'=4,'roll'=2,'head'=4] {'seq','roll'}, dimensions={0}, use_global_device_ids=true | all-gather | bytes 589824 | tf_op jit(solution)/shard_map/all_gather | solution.py:108
  101.5 2.8 fusion.100
  107.1 1.1 copy-done.5
  108.3 2.8 fusion.85
  111.1 15.2 %all-gather.1 = bf16[1,768,2,128]{3,1,2,0:T(8,128)(2,1)} all-gather(bf16[1,192,2,128]{3,1,2,0:T(8,128)(2,1)S(1)} %copy.37), channel_id=3, replica_groups=mesh['seq'=4,'roll'=2,'head'=4] {'seq'}, dimensions={1}, use_global_device_ids=true | all-gather | bytes 491520 | tf_op jit(solution)/shard_map/all_gather | solution.py:139
  127.3 3.9 %while.52 = (s32[]{:T(128)}, f32[2,8,192]{2,1,0:T(8,128)S(1)}, f32[2,8,192,128]{3,2,1,0:T(8,128)S(1)}, s32[]{:T(128)}, pred[]{:T(512)}, /*index=5*/bf16[768,2,12...) while((s32[]{:T(128)}, f32[2,8,192]{2,1,0:T(8,128)S(1)}, ...), condition=%wide.region_17.18_spmd.clone, body=%wide.region_13.17_spmd.clone.sunk | while | flops 409387456 | bytes 10718524 | solution.py:176
  127.3 3.7 %conditional.10 = ((f32[2,8,192]{2,1,0:T(8,128)S(1)}, f32[2,8,192,128]{3,2,1,0:T(8,128)S(1)})) conditional(s32[]{:T(128)} %convert_element_type.194, (f32[2,8,192]{2,1,0:T(8,128)S(1)}, f32[2,8,192,128]{3,2,1,0:T(8,128)S(1)}) %tuple.157, (s32[]{:T(128)}, s32[256]{0:T(256)S(1)}, s32[]{:T(128)}, bf16[768,2,128]{2,0,1:T(8,128)(2,1)S(1)}, ...), branch_computations={%region_14.14_spmd, %region_15.16_spmd} | conditional | flops 409387456 | bytes 10716490 | solution.py:167
  127.5 1.4 fusion.13
  128.9 2.1 fusion.20
  131.2 1.5 copy.39
  132.7 2.6 fusion.108
  135.4 1.2 fusion.120
  136.6 1.2 fusion.123
  138.5 1.2 fusion.126
  140.4 1.2 fusion.129
  141.6 1.2 pad_maximum_fusion.1
  143.1 2.8 fusion.62
  145.9 1.1 copy-done.19
  147.8 1.1 fusion.68
  149.7 1.1 fusion.71
  151.6 1.1 fusion.65
  152.7 1.2 copy-done.15
  154.6 1.1 pad_maximum_fusion
  155.7 2.1 fusion.134
  157.9 1.6 fusion.133
  160.1 1.7 add_bitcast_fusion
  161.8 0.9 broadcast_in_dim.191
  163.7 10.8 %while.53 = (s32[]{:T(128)}, f32[192,2,8,128]{3,0,2,1:T(8,128)}, f32[768,2,128]{2,0,1:T(8,128)}, f32[768,2,128]{2,0,1:T(8,128)}, s32[]{:T(128)}, /*index=5*/pred...) while((s32[]{:T(128)}, f32[192,2,8,128]{3,0,2,1:T(8,128)}, ...), condition=%wide.region_22.23_spmd.clone, body=%wide.region_19.22_spmd.clone.sunk | while | flops 1015726528 | bytes 34195984 | solution.py:239
  164.8 7.4 %conditional.11 = ((f32[192,2,8,128]{3,0,2,1:T(8,128)}, f32[768,2,128]{2,0,1:T(8,128)}, f32[768,2,128]{2,0,1:T(8,128)})) conditional(s32[]{:T(128)} %convert_element_type.195, (f32[192,2,8,128]{3,0,2,1:T(8,128)}, f32[768,2,128]{2,0,1:T(8,128)}, f32[768,2,128]{2,0,1:T(8,128)}) %tuple.160, (s32[]{:T(128)}, s32[256]{0:T(256)}, s32[]{:T(128)}, ...), branch_computations={%region_20.20_spmd, %region_21.21_spmd} | conditional | flops 1015726528 | bytes 34193896 | solution.py:231
  165.6 2.5 fusion.34
  168.8 1.5 fusion.41
  170.3 2.0 fusion.45
  174.5 1.9 copy.49
  176.4 1.8 copy.50
  178.3 1.4 copy.86
  180.9 67.4 %all-reduce.4 = (bf16[768,2,128]{2,1,0:T(2,128)(2,1)S(1)}, bf16[768,2,128]{2,1,0:T(2,128)(2,1)}) all-reduce(f32[768,2,128]{2,1,0:T(2,128)S(1)} %copy.49, f32[768,2,128]{2,1,0:T(2,128)S(1)} %copy.50), channel_id=4, replica_groups=mesh['seq'=4,'roll'=2,'head'=4] {'seq'}, use_global_device_ids=true, to_apply=%region_23.24.clone | all-reduce | flops 393216 | bytes 2359296
  248.4 1.7 fusion.136
  250.6 2.1 fusion.109
  254.4 31.5 %reduce-scatter.3.cloned.1.call-done = f32[128,2,128]{2,0,1:T(8,128)} async-done(((f32[1024,2,128]{2,0,1:T(8,128)}), f32[128,2,128]{2,0,1:T(8,128)}) %reduce-scatter.3.cloned.1.call-update) | async-done | bytes 131088 | tf_op jit(solution)/shard_map/reduce_scatter | solution.py:247
  (137 shorter events, 21.4 us)
Async XLA Ops:
  7.2 245.5 %reduce-scatter.5.cloned.1.call-start = ((), (), s32[]{:S(2)}) async-start(), calls=%async_computation.3 | async-start | bytes 1179648 | tf_op jit(solution)/shard_map/reduce_scatter | solution.py:248
  42.4 7.0 %copy-start.21 = (bf16[1024,2,128]{2,0,1:T(8,128)(2,1)}, bf16[1024,2,128]{2,0,1:T(8,128)(2,1)S(1)}, u32[]{:S(2)}) copy-start(bf16[1024,2,128]{2,0,1:T(8,128)(2,1)S(1)} %all_gather.12) | copy-start | bytes 1572868
  47.1 5.3 %copy-start.29 = (bf16[1,192,2,128]{3,2,1,0:T(2,128)(2,1)S(1)}, bf16[1,192,2,128]{3,2,1,0:T(2,128)(2,1)}, u32[]{:S(2)}) copy-start(bf16[1,192,2,128]{3,2,1,0:T(2,128)(2,1)} %param.20) | copy-start | bytes 294916
  66.9 1.3 copy-start.31
  68.1 36.2 %copy-start = (f32[2,256,192,8]{1,2,3,0:T(8,128)S(1)}, f32[2,256,192,8]{1,2,3,0:T(8,128)}, u32[]{:S(2)}) copy-start(f32[2,256,192,8]{1,2,3,0:T(8,128)} %get-tuple-element.1044) | copy-start | bytes 9437188
  101.5 24.9 %copy-start.23 = (bf16[1024,2,128]{2,0,1:T(8,128)(2,1)}, bf16[1024,2,128]{2,0,1:T(8,128)(2,1)S(1)}, u32[]{:S(2)}) copy-start(bf16[1024,2,128]{2,0,1:T(8,128)(2,1)S(1)} %all_gather.14) | copy-start | bytes 1572868
  104.3 1.9 copy-start.3
  104.3 2.8 copy-start.8
  105.2 3.0 %copy-start.5 = (f32[2,256,192,8]{1,2,3,0:T(8,128)S(1)}, f32[2,256,192,8]{1,2,3,0:T(8,128)}, u32[]{:S(2)}) copy-start(f32[2,256,192,8]{1,2,3,0:T(8,128)} %get-tuple-element.1048) | copy-start | bytes 9437188
  108.3 2.8 copy-start.30
  131.2 1.6 copy-start.25
  131.2 4.2 %copy-start.9 = (f32[2,256,192,8]{1,2,3,0:T(8,128)S(1)}, f32[2,256,192,8]{1,2,3,0:T(8,128)}, u32[]{:S(2)}) copy-start(f32[2,256,192,8]{1,2,3,0:T(8,128)} %get-tuple-element.1046) | copy-start | bytes 9437188
  131.2 5.3 %copy-start.34 = (pred[192]{0:T(512)(128)(4,1)}, pred[192]{0:T(512)(128)(4,1)S(1)}, u32[]{:S(2)}) copy-start(pred[192]{0:T(512)(128)(4,1)S(1)} %fusion.139) | copy-start | bytes 580
  132.7 3.8 %copy-start.6 = (f32[2,256,192,8]{1,2,3,0:T(8,128)S(1)}, f32[2,256,192,8]{1,2,3,0:T(8,128)}, u32[]{:S(2)}) copy-start(f32[2,256,192,8]{1,2,3,0:T(8,128)} %get-tuple-element.1048) | copy-start | bytes 9437188
  136.6 1.9 copy-start.1
  138.5 1.9 copy-start.4
  142.7 143.1 %reduce-scatter.3.cloned.1.call-start = ((), (), s32[]{:S(2)}) async-start(), calls=%async_computation.2 | async-start | bytes 1179648 | tf_op jit(solution)/shard_map/reduce_scatter | solution.py:247
  143.0 4.8 %copy-start.7 = (f32[2,256,192,8]{1,2,3,0:T(8,128)S(1)}, f32[2,256,192,8]{1,2,3,0:T(8,128)}, u32[]{:S(2)}) copy-start(f32[2,256,192,8]{1,2,3,0:T(8,128)} %get-tuple-element.1048) | copy-start | bytes 9437188
  143.0 4.8 %copy-start.24 = (bf16[1024,2,128]{2,0,1:T(8,128)(2,1)S(1)}, bf16[1024,2,128]{2,0,1:T(8,128)(2,1)}, u32[]{:S(2)}) copy-start(bf16[1024,2,128]{2,0,1:T(8,128)(2,1)} %copy-done.23) | copy-start | bytes 1572868
  143.0 4.7 %copy-start.27 = (f32[2,8,192]{2,1,0:T(8,128)S(1)}, f32[2,8,192]{2,1,0:T(8,128)}, u32[]{:S(2)}) copy-start(f32[2,8,192]{2,1,0:T(8,128)} %get-tuple-element.1328) | copy-start | bytes 36868
  145.9 1.1 copy-start.19
  147.8 1.9 copy-start.10
  148.9 1.9 copy-start.14
  149.7 1.9 copy-start.2
  150.8 1.9 copy-start.17
  152.7 1.2 copy-start.15
  155.7 2.2 copy-start.18
  155.7 3.8 %copy-start.16 = (bf16[2,8,192,256]{3,2,1,0:T(8,128)(2,1)S(1)}, bf16[2,8,192,256]{3,2,1,0:T(8,128)(2,1)}, u32[]{:S(2)}) copy-start(bf16[2,8,192,256]{3,2,1,0:T(8,128)(2,1)} %copy-done.15) | copy-start | bytes 4718596
  155.7 3.8 %copy-start.22 = (bf16[1024,2,128]{2,0,1:T(8,128)(2,1)S(1)}, bf16[1024,2,128]{2,0,1:T(8,128)(2,1)}, u32[]{:S(2)}) copy-start(bf16[1024,2,128]{2,0,1:T(8,128)(2,1)} %copy-done.21) | copy-start | bytes 1572868
  157.9 2.2 copy-start.20
  164.8 0.7 copy-start.32
  164.8 0.7 copy-start.33
  164.8 0.8 copy-start.28
  165.6 2.6 copy-start.11
  168.8 3.5 %copy-start.12 = (f32[192,2,8,128]{3,0,2,1:T(8,128)}, f32[192,2,8,128]{3,0,2,1:T(8,128)S(1)}, u32[]{:S(2)}) copy-start(f32[192,2,8,128]{3,0,2,1:T(8,128)S(1)} %bitcast_add_fusion) | copy-start | bytes 4718596 | tf_op jit(solution)/shard_map/while/body/eval_jaxpr/cond
  174.5 3.6 %copy-start.13 = (f32[192,2,8,128]{3,0,2,1:T(8,128)S(1)}, f32[192,2,8,128]{3,0,2,1:T(8,128)}, u32[]{:S(2)}) copy-start(f32[192,2,8,128]{3,0,2,1:T(8,128)} %get-tuple-element.873) | copy-start | bytes 4718596
  176.4 3.3 %copy-start.35 = (u32[32]{0:T(128)S(1)}, u32[32]{0:T(128)}, u32[]{:S(2)}) copy-start(u32[32]{0:T(128)} %constant.188) | copy-start | bytes 388
  178.1 71.9 %copy-start.26 = (f32[2,8,192]{2,1,0:T(8,128)S(1)}, f32[2,8,192]{2,1,0:T(8,128)}, u32[]{:S(2)}) copy-start(f32[2,8,192]{2,1,0:T(8,128)} %copy-done.25) | copy-start | bytes 36868
Sparse Core Ops, SparseCore 0:
  142.9 75.0 reduce-scatter.4
  221.7 64.1 reduce-scatter.2
where the time goes:
time: 295 us; the launch traced here: 294 us
  blocking collectives  163 us (55%)
  matrix products  46.1 us (16%)
  waiting for transfers between devices  31.5 us (11%)
  local copies, waits for them, and re-layouts  23.8 us (8%)
  between operations  16 us (5%)
  other arithmetic  12.6 us (4%)
    unnamed x1, blocking collectives  67.4 us
    all_gather x1, blocking collectives, local(): lax.all_gather(prompt_values, ('seq', 'roll'), axis=0, tiled=True)  33.3 us
    all_gather x1, blocking collectives, local(): lax.all_gather(prompt_keys, ('seq', 'roll'), axis=0, tiled=True)  33 us
    reduce_scatter x1, waiting for transfers between devices, local(): lax.psum_scatter(prompt_key_terms, ('seq', 'roll'), scatter_dimension=0,...  31.5 us
    all_gather x1, blocking collectives, local(): lax.all_gather(own_values, 'seq', axis=0, tiled=True)  15.2 us
    all_gather x1, blocking collectives, local(): lax.all_gather(own_keys, 'seq', axis=0, tiled=True)  14.4 us
    dot_general x7, matrix products, scores_for(): jnp.einsum('ngqd,kgd->gqnk', query_grid, key_block, preferred_element_typ...  12.2 us
    unnamed x71, local copies, waits for them, and re-layouts  11.7 us
  transfers between devices with their start and end apart: 2, of which 1 were waited for; matrix products, arithmetic and copies ran while one was open for 14% of the time, Pallas kernels for 0%

commit v1 on v0

v1 whole, which is shorter than its diff:
```python
import math

import jax
import jax.numpy as jnp
from jax import lax
from jax.experimental import pallas as pl
from jax.experimental.pallas import tpu as pltpu
from jax.sharding import PartitionSpec as P

BF16 = jnp.bfloat16
F32 = jnp.float32
LOG2E = math.log2(math.e)
VMEM = pl.BlockSpec(memory_space=pltpu.VMEM)
SMEM = pl.BlockSpec(memory_space=pltpu.SMEM)
HBM = pl.BlockSpec(memory_space=pltpu.HBM)


def dot_nn(a, b):
    return lax.dot_general(a, b, (((1,), (0,)), ((), ())), preferred_element_type=F32)


def dot_nt(a, b):
    return lax.dot_general(a, b, (((1,), (1,)), ((), ())), preferred_element_type=F32)


def params(mib=32):
    return pltpu.CompilerParams(vmem_limit_bytes=mib * 1024 * 1024)


def cost(flops, read_written, exps=0):
    return pl.CostEstimate(flops=flops, bytes_accessed=read_written, transcendentals=exps)


def load_all(refs, buffers, sems):
    copies = [pltpu.make_async_copy(ref, buffer, sems.at[i]) for i, (ref, buffer) in enumerate(zip(refs, buffers))]
    for copy in copies:
        copy.start()
    return copies


def split_heads(*arrays):
    groups, dim = arrays[0].shape[1:]
    starts = [0]
    for array in arrays:
        starts.append(starts[-1] + array.shape[0])

    def body(*refs):
        ins, outs = refs[: len(arrays)], refs[len(arrays) : len(arrays) + groups]
        buffers, sems = refs[len(arrays) + groups : -1], refs[-1]
        copies = load_all(ins, buffers, sems)
        for i, (copy, buffer) in enumerate(zip(copies, buffers)):
            copy.wait()
            wide = buffer[...].astype(F32)
            for g in range(groups):
                outs[g][starts[i] : starts[i + 1], :] = wide[:, g, :].astype(BF16)

    return pl.pallas_call(
        body,
        out_shape=[jax.ShapeDtypeStruct((starts[-1], dim), BF16)] * groups,
        in_specs=[HBM] * len(arrays),
        out_specs=[VMEM] * groups,
        scratch_shapes=[pltpu.VMEM(a.shape, BF16) for a in arrays] + [pltpu.SemaphoreType.DMA((len(arrays),))],
        compiler_params=params(63),
        cost_estimate=cost(0, 8 * starts[-1] * dim * groups),
    )(*arrays)


def split_queries(scalars, queries, grad_out, groups, own):
    rows, heads, dim = queries.shape
    per = heads // groups
    flat = rows * per

    def body(scalar_ref, q_ref, do_ref, *refs):
        own_refs, outs = refs[: len(own)], refs[len(own) :]
        wide = q_ref[...].astype(F32)
        for g in range(groups):
            outs[g][...] = wide[:, g * per : (g + 1) * per, :].reshape(flat, dim).astype(BF16)
        seen = lax.broadcasted_iota(jnp.int32, (rows, 1, 1), 0) < scalar_ref[0]
        wide = jnp.where(seen, do_ref[...].astype(F32), 0.0)
        for g in range(groups):
            outs[groups + g][...] = wide[:, g * per : (g + 1) * per, :].reshape(flat, dim).astype(BF16)
        for ref, out in zip(own_refs, outs[2 * groups :]):
            out[...] = ref[...]

    shapes = [jax.ShapeDtypeStruct((flat, dim), BF16)] * (2 * groups)
    shapes += [jax.ShapeDtypeStruct(item.shape, item.dtype) for item in own]
    outs = pl.pallas_call(
        body,
        out_shape=shapes,
        in_specs=[SMEM] + [VMEM] * (2 + len(own)),
        out_specs=[VMEM] * len(shapes),
        compiler_params=params(),
        cost_estimate=cost(0, 16 * rows * heads * dim),
    )(scalars, queries, grad_out, *own)
    return outs[:groups], outs[groups : 2 * groups], outs[2 * groups :]


def attend(scalars, queries, cotangent, prompts, rollouts, roll_size, block, first, end, carry):
    flat, dim = queries.shape
    seq_size = len(rollouts)
    prow, rrow = prompts[0][2] // 2, rollouts[0][2] // 2
    per = flat // rrow
    prompt_total = prow * seq_size * roll_size
    total = prompt_total + rrow * seq_size
    here = (end - first) * block
    opening, closing = first == 0, end * block == flat
    scale = dim ** (-0.5)
    exponent = scale * LOG2E
    sources, places = list(carry), []
    for array, at, rows in prompts + rollouts if opening else []:
        known = [i for i, seen in enumerate(sources) if seen is array]
        if not known:
            known = [len(sources)]
            sources.append(array)
        places.append((known[0], at, rows // 2))

    def body(*refs):
        scalar_ref, q_ref, do_ref = refs[:3]
        source_refs = refs[3 : 3 + len(sources)]
        out_ref, ds_ref = refs[3 + len(sources) : 5 + len(sources)]
        rest = list(refs[5 + len(sources) :])
        if opening:
            k_s, v_s = rest.pop(0), rest.pop(0)
        else:
            k_s, v_s = source_refs[:2]
        if closing:
            line_refs, grad_refs = rest[:roll_size], rest[roll_size : roll_size + seq_size]
        dk_s, dv_s = rest[-2:]
        live = scalar_ref[0]
        rank = scalar_ref[1]

        lower = 0
        for which, start, rows in places:
            k_s[lower : lower + rows, :] = source_refs[which][start : start + rows, :]
            v_s[lower : lower + rows, :] = source_refs[which][start + rows : start + 2 * rows, :]
            lower += rows
        if opening:
            dk_s[...] = jnp.zeros_like(dk_s)
            dv_s[...] = jnp.zeros_like(dv_s)
        else:
            dk_s[...] = source_refs[2][...]
            dv_s[...] = source_refs[3][...]

        column = lax.broadcasted_iota(jnp.int32, (1, rrow * seq_size), 1)
        key_at = column
        for slot in range(1, seq_size):
            key_at = jnp.where(column >= slot * rrow, column + (scalar_ref[1 + slot] - rank - slot) * rrow, key_at)

        def forward(step):
            span = slice(step * block, (step + 1) * block)
            row = (step * block + lax.broadcasted_iota(jnp.int32, (block, 1), 0)) // per
            q = q_ref[span, :]
            s_p = dot_nt(q, k_s[:prompt_total, :])
            s_r = dot_nt(q, k_s[prompt_total:, :])
            s_r = jnp.where(key_at <= row, s_r, -jnp.inf)
            top = jnp.maximum(jnp.max(s_p, axis=1, keepdims=True), jnp.max(s_r, axis=1, keepdims=True))
            e_p = jnp.exp2((s_p - top) * exponent)
            e_r = jnp.exp2((s_r - top) * exponent)
            sums = jnp.sum(e_p, axis=1, keepdims=True) + jnp.sum(e_r, axis=1, keepdims=True)
            p_p = e_p.astype(BF16)
            p_r = e_r.astype(BF16)
            o = (dot_nn(p_p, v_s[:prompt_total, :]) + dot_nn(p_r, v_s[prompt_total:, :])) / sums
            there = slice((step - first) * block, (step - first + 1) * block)
            out_ref[there, :] = jnp.where(row < live, o, 0.0).astype(BF16)
            cot = (do_ref[span, :].astype(F32) * (scale / sums)).astype(BF16)
            cot32 = cot.astype(F32)
            off = jnp.sum(cot32 * o, axis=1, keepdims=True)
            q_t = q.astype(F32).T.astype(BF16)
            cot_t = cot32.T.astype(BF16)
            return p_p, p_r, cot, off, q_t, cot_t

        def backward(step, state):
            there = slice((step - first) * block, (step - first + 1) * block)
            p_p, p_r, cot, off, q_t, cot_t = state
            dv_s[:, :prompt_total] += dot_nn(cot_t, p_p)
            dv_s[:, prompt_total:] += dot_nn(cot_t, p_r)
            ds_p = (p_p.astype(F32) * (dot_nt(cot, v_s[:prompt_total, :]) - off)).astype(BF16)
            ds_r = (p_r.astype(F32) * (dot_nt(cot, v_s[prompt_total:, :]) - off)).astype(BF16)
            ds_ref[there, :prompt_total] = ds_p
            ds_ref[there, prompt_total:] = ds_r
            dk_s[:, :prompt_total] += dot_nn(q_t, ds_p)
            dk_s[:, prompt_total:] += dot_nn(q_t, ds_r)

        state = forward(first)
        for step in range(first, end):
            ahead = forward(step + 1) if step + 1 < end else None
            backward(step, state)
            state = ahead
        if not closing:
            return

        dk = dk_s[...].T
        dv = dv_s[...].T * (1.0 / scale)
        for dx, ref in enumerate(line_refs):
            for slot in range(seq_size):
                lower = (dx * seq_size + slot) * prow
                at = 2 * slot * prow
                ref[at : at + prow, :] = dk[lower : lower + prow, :].astype(ref.dtype)
                ref[at + prow : at + 2 * prow, :] = dv[lower : lower + prow, :].astype(ref.dtype)
        for slot, ref in enumerate(grad_refs):
            lower = prompt_total + slot * rrow
            ref[:rrow, :] = dk[lower : lower + rrow, :].astype(ref.dtype)
            ref[rrow:, :] = dv[lower : lower + rrow, :].astype(ref.dtype)

    shapes = [((here, dim), BF16), ((here, total), BF16)]
    sums = [((dim, total), F32)] * 2
    if opening:
        shapes += [((total, dim), BF16)] * 2
    if closing:
        shapes += [((seq_size * 2 * prow, dim), BF16 if dx else F32) for dx in range(roll_size)]
        shapes += [((2 * rrow, dim), BF16 if slot else F32) for slot in range(seq_size)]
    else:
        shapes += sums
    outs = pl.pallas_call(
        body,
        out_shape=[jax.ShapeDtypeStruct(shape, kind) for shape, kind in shapes],
        in_specs=[SMEM] + [VMEM] * (2 + len(sources)),
        out_specs=[VMEM] * len(shapes),
        scratch_shapes=[pltpu.VMEM(shape, kind) for shape, kind in sums] if closing else [],
        compiler_params=params(),
        cost_estimate=cost(20 * here * total * dim, 16 * here * dim, here * total),
    )(scalars, queries, cotangent, *sources)
    part, rest = tuple(outs[:2]), list(outs[2:])
    if not closing:
        return part, rest
    keys, rest = (rest[0], rest[2:]) if opening else (carry[0], rest)
    return part, keys, rest[:roll_size], rest[roll_size:]


def row_outputs(heads, keys, rows, block):
    groups = len(heads)
    total, dim = keys[0].shape
    flat = sum(out.shape[0] for out, _ in heads[0])
    per = flat // rows
    arrays = [item for head in heads for part in head for item in part]
    where, at = [], 0
    for head in heads:
        where.append([])
        for out, _ in head:
            where[-1] += [(at, lower) for lower in range(0, out.shape[0], block)]
            at += 2

    def body(*refs):
        part_refs, k_refs = refs[: len(arrays)], refs[len(arrays) : len(arrays) + groups]
        attention_ref, dq_ref = refs[len(arrays) + groups :]
        for i in range(flat // block):
            there = slice(i * block // per, (i + 1) * block // per)
            outs, grads = [], []
            for places, k in zip(where, k_refs):
                at, lower = places[i]
                span = slice(lower, lower + block)
                outs.append(part_refs[at][span, :].astype(F32).reshape(block // per, per, dim))
                grads.append(dot_nn(part_refs[at + 1][span, :], k[...]).reshape(block // per, per, dim))
            attention_ref[there] = jnp.concatenate(outs, axis=1).astype(BF16)
            dq_ref[there] = jnp.concatenate(grads, axis=1).astype(BF16)

    return pl.pallas_call(
        body,
        out_shape=[jax.ShapeDtypeStruct((rows, per * groups, dim), BF16)] * 2,
        in_specs=[VMEM] * (len(arrays) + groups),
        out_specs=[VMEM] * 2,
        compiler_params=params(),
        cost_estimate=cost(4 * groups * flat * total * dim, 2 * groups * flat * total),
    )(*arrays, *keys)


def pair_sum(owns, received, seq_size):
    groups = len(owns)
    rows, dim = owns[0].shape
    part = rows // seq_size
    count = len(received[0])

    def body(*refs):
        own_refs, other_refs, outs = refs[:groups], refs[groups : groups * (1 + count)], refs[groups * (1 + count) :]
        for slot, out in enumerate(outs):
            span = slice(slot * part, (slot + 1) * part)
            for g, own_ref in enumerate(own_refs):
                value = own_ref[span, :]
                for other in other_refs[g * count : (g + 1) * count]:
                    value = value + other[span, :].astype(F32)
                out[g * part : (g + 1) * part, :] = value.astype(out.dtype)

    return pl.pallas_call(
        body,
        out_shape=[jax.ShapeDtypeStruct((groups * part, dim), BF16 if slot else F32) for slot in range(seq_size)],
        in_specs=[VMEM] * (groups * (1 + count)),
        out_specs=[VMEM] * seq_size,
        compiler_params=params(),
        cost_estimate=cost(groups * rows * dim, groups * rows * dim * 10),
    )(*owns, *[item for line in received for item in line])


def finish(owns, received, groups):
    each = groups // len(owns)
    dim = owns[0].shape[1]
    rows = owns[0].shape[0] // (2 * each)
    count = len(received[0])

    def body(*refs):
        own, rest = refs[: len(owns)], refs[len(owns) :]
        sums = []
        for g in range(groups):
            i, span = g // each, slice(g % each * 2 * rows, (g % each + 1) * 2 * rows)
            value = own[i][span, :]
            for other in rest[i * count : (i + 1) * count]:
                value = value + other[span, :].astype(F32)
            sums.append(value)
        for part, out in enumerate(refs[-2:]):
            pieces = [value[part * rows : (part + 1) * rows, None, :] for value in sums]
            out[...] = jnp.concatenate(pieces, axis=1).astype(BF16)

    flat = [item for line in received for item in line]
    return pl.pallas_call(
        body,
        out_shape=[jax.ShapeDtypeStruct((rows, groups, dim), BF16)] * 2,
        in_specs=[VMEM] * (len(owns) + len(flat)),
        out_specs=[VMEM] * 2,
        compiler_params=params(),
        cost_estimate=cost(2 * rows * groups * dim * count, 2 * rows * groups * dim * 10),
    )(*owns, *flat)


def after(value, *others):
    return lax.optimization_barrier((value, others))[0]


def local(queries, rollout_keys, rollout_values, prompt_keys, prompt_values, grad_out, lengths):
    seq_size, roll_size = lax.axis_size("seq"), lax.axis_size("roll")
    row_count, groups = queries.shape[1], prompt_keys.shape[1]
    flat = row_count * queries.shape[2] // groups
    rank = lax.axis_index("seq")
    paired = seq_size & (seq_size - 1) == 0
    slots = range(1, seq_size)
    origin = [(rank ^ slot) if paired else (rank - slot) % seq_size for slot in slots]
    scalars = jnp.stack([lengths[0] - rank * row_count, rank] + origin).astype(jnp.int32)

    def pairs(slot):
        return [(i, i ^ slot if paired else (i + slot) % seq_size) for i in range(seq_size)]

    def over_seq(value, which):
        return lax.ppermute(value, "seq", which)

    def give_back(value, slot):
        return over_seq(value, [(b, a) for a, b in pairs(slot)])

    def give_down(value, slot):
        return over_seq(value, [(b, a) for a, b in pairs(slot) if a < b])

    def over_roll(value, shift):
        return lax.ppermute(value, "roll", [(i, (i + shift) % roll_size) for i in range(roll_size)])

    own = split_heads(prompt_keys, prompt_values, rollout_keys[0], rollout_values[0])
    q_groups, cot_groups, kept = split_queries(scalars, queries[0], grad_out[0], groups, own)
    prows, rrows = 2 * prompt_keys.shape[0], 2 * row_count

    def send_over_seq(part, same):
        return [same] + [over_seq(part, pairs(slot)) for slot in slots]

    def send_over_roll(messages):
        line = jnp.concatenate([item[:prows] for item in messages], axis=0)
        return [line] + [over_roll(line, shift) for shift in range(1, roll_size)]

    messages = send_over_seq(own[0], kept[0])
    lines = send_over_roll(messages)
    block = math.gcd(flat, 256)
    steps = flat // block
    heads, all_keys, line_own, line_got, roll_own, roll_got = [], [], [], [], [], []
    for g in range(groups):
        prompts = [(item, slot * prows, prows) for item in lines for slot in range(seq_size)]
        rollouts = [(item, prows, rrows) for item in messages]
        if g + 1 < groups:
            messages = send_over_seq(after(own[g + 1], lines[0]), kept[g + 1])
        cuts = [0, steps // 2, steps] if g else [0, steps]
        parts, carry = [], []
        for start, stop in zip(cuts, cuts[1:]):
            if start:
                carry = [after(item, roll_got[g - 1]) for item in carry]
            part, *rest = attend(
                scalars, q_groups[g], cot_groups[g], prompts, rollouts, roll_size, block, start, stop, carry
            )
            parts.append(part)
            carry = rest[0]
        keys, line_grads, roll_grads = rest
        heads.append(parts)
        all_keys.append(keys)
        line_own.append(line_grads[0])
        line_got.append([over_roll(line_grads[shift], -shift) for shift in range(1, roll_size)])
        if g + 1 < groups:
            messages = [after(item, parts) for item in messages]
            lines = send_over_roll(messages)
            roll_grads = [after(item, lines[0]) for item in roll_grads]
        roll_own.append(roll_grads[0])
        roll_got.append([give_down(roll_grads[slot], slot) for slot in slots])

    sums = pair_sum(line_own, line_got, seq_size)
    attention_rows, grad_rows = row_outputs(heads, all_keys, row_count, block)
    grad_rk, grad_rv = finish(roll_own, roll_got, groups)
    grad_pk, grad_pv = finish([sums[0]], [[give_back(sums[slot], slot) for slot in slots]], groups)
    return attention_rows[None], grad_rows[None], grad_rk[None], grad_rv[None], grad_pk, grad_pv


def solution(mesh):
    rows = P("roll", "seq", "head", None)
    shared = P(("seq", "roll"), "head", None)
    return jax.shard_map(
        local,
        mesh=mesh,
        in_specs=(rows, rows, rows, shared, shared, rows, P("roll")),
        out_specs=(rows, rows, rows, rows, shared, shared),
        check_vma=False,
    )
```

time: 295 us -> 84.3 us (0.29)
  blocking collectives: 163 us -> 0 us
  matrix products: 46.1 us -> 0 us
  starting transfers between devices: 0.3 us -> 29 us
  Pallas kernels: 0 us -> 28.2 us
  local copies, waits for them, and re-layouts: 23.8 us -> 3.31 us
  between operations: 16 us -> 1.49 us
  other arithmetic: 12.6 us -> 0.04 us
  waiting for transfers between devices: 31.5 us -> 21.9 us
    all_gather x4 -> x0, blocking collectives: 96 us -> none  [the longest x1 33.3 us: local(): lax.all_gather(prompt_values, ('seq', 'roll'), axis=0, tiled=True)]
    unnamed x1 -> x0, blocking collectives: 67.4 us -> none
    dot_general x32 -> x0, matrix products: 46.1 us -> none  [the longest x7 12.2 us: scores_for(): jnp.einsum('ngqd,kgd->gqnk', query_grid, key_block, preferred_element_typ...]
    reduce_scatter x2 -> x0, waiting for transfers between devices: 31.5 us -> none  [the longest x1 31.5 us: local(): lax.psum_scatter(prompt_key_terms, ('seq', 'roll'), scatter_dimension=0,...]
    ppermute x0 -> x19, starting transfers between devices: none -> 29 us  [the longest x15 23.8 us: over_seq(): return lax.ppermute(value, 'seq', which)]
    pallas_call x0 -> x9, Pallas kernels: none -> 28.2 us  [the longest x3 18.6 us: attend(): pl.pallas_call(body, out_shape=[jax.ShapeDtypeStruct(shape, kind) for sha...]
    ppermute x0 -> x19, waiting for transfers between devices: none -> 21.9 us  [the longest x15 17.4 us: over_seq(): return lax.ppermute(value, 'seq', which)]
    unnamed x71 -> x6, local copies, waits for them, and re-layouts: 11.7 us -> 3.18 us
  transfers between devices with their start and end apart: 2 -> 19, of which waited for: 1 -> 8; matrix products, arithmetic and copies ran while one was open for 14% -> 0% of each run, Pallas kernels for 0% -> 30%
where the time goes in v1:
time: 84.3 us; the launch traced here: 83.9 us
  starting transfers between devices  29 us (34%)
  Pallas kernels  28.2 us (33%)
  waiting for transfers between devices  21.9 us (26%)
  local copies, waits for them, and re-layouts  3.31 us (4%)
  between operations  1.49 us (2%)
    ppermute x15, starting transfers between devices, over_seq(): return lax.ppermute(value, 'seq', which)  23.8 us
    pallas_call x3, Pallas kernels, attend(): pl.pallas_call(body, out_shape=[jax.ShapeDtypeStruct(shape, kind) for sha...  18.6 us
    ppermute x15, waiting for transfers between devices, over_seq(): return lax.ppermute(value, 'seq', which)  17.4 us
    ppermute x4, starting transfers between devices, over_roll(): lax.ppermute(value, 'roll', [(i, (i + shift) % roll_size) for i in range(...  5.26 us
    ppermute x4, waiting for transfers between devices, over_roll(): lax.ppermute(value, 'roll', [(i, (i + shift) % roll_size) for i in range(...  4.48 us
    pallas_call x1, Pallas kernels, row_outputs(): pl.pallas_call(body, out_shape=[jax.ShapeDtypeStruct((rows, per * groups,...  4.3 us
    unnamed x6, local copies, waits for them, and re-layouts  3.18 us
    pallas_call x1, Pallas kernels, split_heads(): pl.pallas_call(body, out_shape=[jax.ShapeDtypeStruct((starts[-1], dim), B...  2.03 us
  transfers between devices with their start and end apart: 19, of which 8 were waited for; matrix products, arithmetic and copies ran while one was open for 0% of the time, Pallas kernels for 30%

profile of v1, /device:TPU:0, one launch (start us, length us, event | category | flops | bytes accessed | tf_op | source)
XLA Modules:
  0.0 83.9 jit_solution(15607244651546918063)
XLA Ops:
  0.6 2.0 %shard_map.118 = (bf16[640,128]{1,0:T(8,128)(2,1)}, bf16[640,128]{1,0:T(8,128)(2,1)}) custom-call(bf16[128,2,128]{2,1,0:T(2,128)(2,1)} %refs_0_.1, bf16[128,2,128]{2,1,0:T(2,128)(2,1)} %refs_1_.1, bf16[192,2,128]{2,1,0:T(2,128)(2,1)} %bitcast.17, bf16[192,2,128]{2,1,0:T(2,128)(2,1)} %bitcast.18), custom_call_target="tpu_custom_call" | custom-call | bytes 1310720 | tf_op jit(solution)/shard_map/pallas_call | solution.py:57
  2.7 5.1 %collective-permute-start.2 = (bf16[640,128]{1,0:T(8,128)(2,1)}, bf16[640,128]{1,0:T(8,128)(2,1)S(1)}, u32[]{:S(2)}, u32[]{:S(2)}) collective-permute-start(bf16[640,128]{1,0:T(8,128)(2,1)} %get-tuple-element.60.refs_0_), channel_id=1, source_target_pairs={{0,24},{8,16},{16,8},{24,0},{1,25},{9,17},{17,9},{25,1},{2,26},{10... | collective-permute-start | bytes 491528 | tf_op jit(solution)/shard_map/ppermute | solution.py:341
  7.8 0.0 collective-permute-start.1
  7.8 0.6 collective-permute-start
  9.1 0.1 stack.23.scalar_ref.refs_0_
  9.2 1.1 %copy-done = bf16[1,192,16,128]{3,2,1,0:T(8,128)(2,1)S(1)} copy-done((bf16[1,192,16,128]{3,2,1,0:T(8,128)(2,1)S(1)}, bf16[1,192,16,128]{3,2,1,0:T(8,128)(2,1)}, u32[]{:S(2)}) %copy-start) | copy-done | bytes 786456
  10.3 1.1 %copy-done.1 = bf16[1,192,16,128]{3,2,1,0:T(8,128)(2,1)S(1)} copy-done((bf16[1,192,16,128]{3,2,1,0:T(8,128)(2,1)S(1)}, bf16[1,192,16,128]{3,2,1,0:T(8,128)(2,1)}, u32[]{:S(2)}) %copy-start.1) | copy-done | bytes 786456
  11.4 0.9 %copy-done.2 = bf16[640,128]{1,0:T(8,128)(2,1)S(1)} copy-done((bf16[640,128]{1,0:T(8,128)(2,1)S(1)}, bf16[640,128]{1,0:T(8,128)(2,1)}, u32[]{:S(2)}) %copy-start.2) | copy-done | bytes 163864
  12.3 1.2 %shard_map.119 = (bf16[1536,128]{1,0:T(8,128)(2,1)S(1)}, bf16[1536,128]{1,0:T(8,128)(2,1)S(1)}, bf16[1536,128]{1,0:T(8,128)(2,1)S(1)}, bf16[1536,128]{1,0:T(8,12...) custom-call(s32[5]{0:T(128)S(1)} %stack.23.scalar_ref.refs_0_, ...), custom_call_target="tpu_custom_call" | custom-call | bytes 6291456 | tf_op jit(solution)/shard_map/pallas_call | solution.py:87
  13.6 0.0 collective-permute-done.2.refs_8_
  13.6 8.2 %collective-permute-done.1.refs_7_ = bf16[640,128]{1,0:T(8,128)(2,1)S(1)} collective-permute-done((bf16[640,128]{1,0:T(8,128)(2,1)}, bf16[640,128]{1,0:T(8,128)(2,1)S(1)}, u32[]{:S(2)}, u32[]{:S(2)}) %collective-permute-start.1) | collective-permute-done | bytes 163872 | tf_op jit(solution)/shard_map/ppermute | solution.py:341
  21.9 0.0 collective-permute-done.refs_6_
  21.9 1.6 %collective-permute-start.3 = (bf16[1024,128]{1,0:T(8,128)(2,1)S(1)}, bf16[1024,128]{1,0:T(8,128)(2,1)S(1)}, u32[]{:S(2)}, u32[]{:S(2)}) collective-permute-start(bf16[1024,128]{1,0:T(8,128)(2,1)S(1)} %pad_maximum_fusion.refs_3_), channel_id=1, source_target_pairs={{0,4},{4,0},{1,5},{5,1},{2,6},{6,2},{3,7},{7,3},{8,12},{12,8},{9,1... | collective-permute-start | bytes 786440 | tf_op jit(solution)/shard_map/ppermute | solution.py:350
  23.5 2.5 %collective-permute-start.6 = (bf16[640,128]{1,0:T(8,128)(2,1)}, bf16[640,128]{1,0:T(8,128)(2,1)S(1)}, u32[]{:S(2)}, u32[]{:S(2)}) collective-permute-start(bf16[640,128]{1,0:T(8,128)(2,1)} %get-tuple-element.71.refs_1_), channel_id=1, source_target_pairs={{0,24},{8,16},{16,8},{24,0},{1,25},{9,17},{17,9},{25,1},{2,26},{10... | collective-permute-start | bytes 491528 | tf_op jit(solution)/shard_map/ppermute | solution.py:341
  26.0 0.0 collective-permute-start.5
  26.0 1.9 %collective-permute-start.4 = (bf16[640,128]{1,0:T(8,128)(2,1)}, bf16[640,128]{1,0:T(8,128)(2,1)S(1)}, u32[]{:S(2)}, u32[]{:S(2)}) collective-permute-start(bf16[640,128]{1,0:T(8,128)(2,1)} %get-tuple-element.71.refs_1_), channel_id=1, source_target_pairs={{0,8},{8,0},{16,24},{24,16},{1,9},{9,1},{17,25},{25,17},{2,10},{10... | collective-permute-start | bytes 491528 | tf_op jit(solution)/shard_map/ppermute | solution.py:341
  27.9 1.5 %collective-permute-done.3.refs_4_ = bf16[1024,128]{1,0:T(8,128)(2,1)S(1)} collective-permute-done((bf16[1024,128]{1,0:T(8,128)(2,1)S(1)}, bf16[1024,128]{1,0:T(8,128)(2,1)S(1)}, u32[]{:S(2)}, u32[]{:S(2)}) %collective-permute-start.3) | collective-permute-done | bytes 262176 | tf_op jit(solution)/shard_map/ppermute | solution.py:350
  29.4 8.9 %shard_map.120 = (bf16[1536,128]{1,0:T(8,128)(2,1)S(1)}, bf16[1536,1792]{1,0:T(8,128)(2,1)S(1)}, bf16[1792,128]{1,0:T(8,128)(2,1)S(1)}, bf16[1792,128]{1,0:T(8,1...) custom-call(s32[5]{0:T(128)S(1)} %stack.23.scalar_ref.refs_0_, ...), custom_call_target="tpu_custom_call" | custom-call | flops 7046430720 | bytes 3145728 | tf_op jit(solution)/shard_map/pallas_call | solution.py:214
  38.2 0.0 collective-permute-done.6.refs_8_
  38.2 0.5 collective-permute-done.5.refs_7_
  38.7 0.0 collective-permute-done.4.refs_6_
  38.8 1.1 %collective-permute-start.7 = (bf16[1024,128]{1,0:T(8,128)(2,1)S(1)}, bf16[1024,128]{1,0:T(8,128)(2,1)S(1)}, u32[]{:S(2)}, u32[]{:S(2)}) collective-permute-start(bf16[1024,128]{1,0:T(8,128)(2,1)S(1)} %pad_maximum_fusion.1.refs_3_), channel_id=1, source_target_pairs={{0,4},{4,0},{1,5},{5,1},{2,6},{6,2},{3,7},{7,3},{8,12},{12,8},{9,1... | collective-permute-start | bytes 786440 | tf_op jit(solution)/shard_map/ppermute | solution.py:350
  39.9 1.3 %collective-permute-start.8 = (bf16[384,128]{1,0:T(8,128)(2,1)S(1)}, bf16[384,128]{1,0:T(8,128)(2,1)S(1)}, u32[]{:S(2)}, u32[]{:S(2)}) collective-permute-start(bf16[384,128]{1,0:T(8,128)(2,1)S(1)} %get-tuple-element.79), channel_id=1, source_target_pairs={{8,0},{24,16},{9,1},{25,17},{10,2},{26,18},{11,3},{27,19},{12,4},{... | collective-permute-start | bytes 294920 | tf_op jit(solution)/shard_map/ppermute | solution.py:341
  41.2 1.3 %collective-permute-start.9 = (bf16[384,128]{1,0:T(8,128)(2,1)S(1)}, bf16[384,128]{1,0:T(8,128)(2,1)S(1)}, u32[]{:S(2)}, u32[]{:S(2)}) collective-permute-start(bf16[384,128]{1,0:T(8,128)(2,1)S(1)} %get-tuple-element.81), channel_id=1, source_target_pairs={{16,0},{24,8},{17,1},{25,9},{18,2},{26,10},{19,3},{27,11},{20,4},{... | collective-permute-start | bytes 294920 | tf_op jit(solution)/shard_map/ppermute | solution.py:341
  42.5 1.5 %collective-permute-start.10 = (bf16[384,128]{1,0:T(8,128)(2,1)S(1)}, bf16[384,128]{1,0:T(8,128)(2,1)S(1)}, u32[]{:S(2)}, u32[]{:S(2)}) collective-permute-start(bf16[384,128]{1,0:T(8,128)(2,1)S(1)} %get-tuple-element.83), channel_id=1, source_target_pairs={{24,0},{16,8},{25,1},{17,9},{26,2},{18,10},{27,3},{19,11},{28,4},{... | collective-permute-start | bytes 294920 | tf_op jit(solution)/shard_map/ppermute | solution.py:341
  44.0 1.1 %collective-permute-start.14 = (bf16[1024,128]{1,0:T(8,128)(2,1)S(1)}, bf16[1024,128]{1,0:T(8,128)(2,1)S(1)}, u32[]{:S(2)}, u32[]{:S(2)}) collective-permute-start(bf16[1024,128]{1,0:T(8,128)(2,1)S(1)} %get-tuple-element.106), channel_id=1, source_target_pairs={{0,4},{4,0},{1,5},{5,1},{2,6},{6,2},{3,7},{7,3},{8,12},{12,8},{9,1... | collective-permute-start | bytes 786440 | tf_op jit(solution)/shard_map/ppermute | solution.py:350
  45.1 2.2 %collective-permute-done.7.refs_4_ = bf16[1024,128]{1,0:T(8,128)(2,1)S(1)} collective-permute-done((bf16[1024,128]{1,0:T(8,128)(2,1)S(1)}, bf16[1024,128]{1,0:T(8,128)(2,1)S(1)}, u32[]{:S(2)}, u32[]{:S(2)}) %collective-permute-start.7) | collective-permute-done | bytes 262176 | tf_op jit(solution)/shard_map/ppermute | solution.py:350
  47.3 4.8 %shard_map.121 = (bf16[768,128]{1,0:T(8,128)(2,1)S(1)}, bf16[768,1792]{1,0:T(8,128)(2,1)S(1)}, bf16[1792,128]{1,0:T(8,128)(2,1)S(1)}, bf16[1792,128]{1,0:T(8,128...) custom-call(s32[5]{0:T(128)S(1)} %stack.23.scalar_ref.refs_0_, ...), custom_call_target="tpu_custom_call" | custom-call | flops 3523215360 | bytes 1572864 | tf_op jit(solution)/shard_map/pallas_call | solution.py:214
  52.1 0.0 collective-permute-done.8.refs_2_
  52.1 0.8 %collective-permute-done.9.refs_3_ = bf16[384,128]{1,0:T(8,128)(2,1)S(1)} collective-permute-done((bf16[384,128]{1,0:T(8,128)(2,1)S(1)}, bf16[384,128]{1,0:T(8,128)(2,1)S(1)}, u32[]{:S(2)}, u32[]{:S(2)}) %collective-permute-start.9) | collective-permute-done | bytes 98336 | tf_op jit(solution)/shard_map/ppermute | solution.py:341
  53.0 0.0 collective-permute-done.10.refs_4_
  53.0 4.9 %shard_map.122 = (bf16[768,128]{1,0:T(8,128)(2,1)S(1)}, bf16[768,1792]{1,0:T(8,128)(2,1)S(1)}, f32[1024,128]{1,0:T(8,128)S(1)}, bf16[1024,128]{1,0:T(8,128)(2,1)...) custom-call(s32[5]{0:T(128)S(1)} %stack.23.scalar_ref.refs_0_, ...), custom_call_target="tpu_custom_call" | custom-call | flops 3523215360 | bytes 1572864 | tf_op jit(solution)/shard_map/pallas_call | solution.py:214
  57.9 1.5 %collective-permute-start.15 = (bf16[1024,128]{1,0:T(8,128)(2,1)S(1)}, bf16[1024,128]{1,0:T(8,128)(2,1)S(1)}, u32[]{:S(2)}, u32[]{:S(2)}) collective-permute-start(bf16[1024,128]{1,0:T(8,128)(2,1)S(1)} %get-tuple-element.107), channel_id=1, source_target_pairs={{0,4},{4,0},{1,5},{5,1},{2,6},{6,2},{3,7},{7,3},{8,12},{12,8},{9,1... | collective-permute-start | bytes 786440 | tf_op jit(solution)/shard_map/ppermute | solution.py:350
  59.4 1.3 %collective-permute-start.11 = (bf16[384,128]{1,0:T(8,128)(2,1)S(1)}, bf16[384,128]{1,0:T(8,128)(2,1)S(1)}, u32[]{:S(2)}, u32[]{:S(2)}) collective-permute-start(bf16[384,128]{1,0:T(8,128)(2,1)S(1)} %get-tuple-element.99), channel_id=1, source_target_pairs={{8,0},{24,16},{9,1},{25,17},{10,2},{26,18},{11,3},{27,19},{12,4},{... | collective-permute-start | bytes 294920 | tf_op jit(solution)/shard_map/ppermute | solution.py:341
  60.7 1.3 %collective-permute-start.12 = (bf16[384,128]{1,0:T(8,128)(2,1)S(1)}, bf16[384,128]{1,0:T(8,128)(2,1)S(1)}, u32[]{:S(2)}, u32[]{:S(2)}) collective-permute-start(bf16[384,128]{1,0:T(8,128)(2,1)S(1)} %get-tuple-element.100), channel_id=1, source_target_pairs={{16,0},{24,8},{17,1},{25,9},{18,2},{26,10},{19,3},{27,11},{20,4},{... | collective-permute-start | bytes 294920 | tf_op jit(solution)/shard_map/ppermute | solution.py:341
  62.0 1.5 %collective-permute-start.13 = (bf16[384,128]{1,0:T(8,128)(2,1)S(1)}, bf16[384,128]{1,0:T(8,128)(2,1)S(1)}, u32[]{:S(2)}, u32[]{:S(2)}) collective-permute-start(bf16[384,128]{1,0:T(8,128)(2,1)S(1)} %get-tuple-element.101), channel_id=1, source_target_pairs={{24,0},{16,8},{25,1},{17,9},{26,2},{18,10},{27,3},{19,11},{28,4},{... | collective-permute-start | bytes 294920 | tf_op jit(solution)/shard_map/ppermute | solution.py:341
  63.5 0.0 collective-permute-done.14.refs_2_
  63.5 0.8 collective-permute-done.15.refs_3_
  64.3 0.1 shard_map.125
  64.4 2.2 %collective-permute-start.16 = (bf16[512,128]{1,0:T(8,128)(2,1)S(1)}, bf16[512,128]{1,0:T(8,128)(2,1)S(1)}, u32[]{:S(2)}, u32[]{:S(2)}) collective-permute-start(bf16[512,128]{1,0:T(8,128)(2,1)S(1)} %get-tuple-element.109), channel_id=1, source_target_pairs={{8,0},{0,8},{24,16},{16,24},{9,1},{1,9},{25,17},{17,25},{10,2},{2,... | collective-permute-start | bytes 393224 | tf_op jit(solution)/shard_map/ppermute | solution.py:341
  66.6 3.3 %collective-permute-start.17 = (bf16[512,128]{1,0:T(8,128)(2,1)S(1)}, bf16[512,128]{1,0:T(8,128)(2,1)S(1)}, u32[]{:S(2)}, u32[]{:S(2)}) collective-permute-start(bf16[512,128]{1,0:T(8,128)(2,1)S(1)} %get-tuple-element.110), channel_id=1, source_target_pairs={{16,0},{24,8},{0,16},{8,24},{17,1},{25,9},{1,17},{9,25},{18,2},{26... | collective-permute-start | bytes 393224 | tf_op jit(solution)/shard_map/ppermute | solution.py:341
  69.9 0.0 collective-permute-start.18
  69.9 4.3 %shard_map.123 = (bf16[192,16,128]{2,1,0:T(8,128)(2,1)}, bf16[192,16,128]{2,1,0:T(8,128)(2,1)}) custom-call(bf16[1536,128]{1,0:T(8,128)(2,1)S(1)} %get-tuple-element.65.refs_0_, bf16[1536,1792]{1,0:T(8,128)(2,1)S(1)} %get-tuple-element.66.refs_1_, bf16[768,128]{1,0:T(8,128)(2,1)S(1)} %get-tuple-element.75.refs_2_, ...), custom_call_target="tpu_custom_call" | custom-call | flops 2818572288 | bytes 11010048 | tf_op jit(solution)/shard_map/pallas_call | solution.py:257
  74.2 0.1 collective-permute-done.12.refs_6_
  74.3 0.0 collective-permute-done.13.refs_7_
  74.3 1.0 %shard_map.124 = (bf16[192,2,128]{2,1,0:T(2,128)(2,1)}, bf16[192,2,128]{2,1,0:T(2,128)(2,1)}) custom-call(f32[384,128]{1,0:T(8,128)S(1)} %get-tuple-element.97.refs_0_, f32[384,128]{1,0:T(8,128)S(1)} %get-tuple-element.98.refs_1_, bf16[384,128]{1,0:T(8,128)(2,1)S(1)} %collective-permute-done.8.refs_2_, bf16[384,128]{1,0:T(8,128)(2,1)S(1)} %collective-permute-done.9.refs_3_, ...), custom_call_target="tpu_custom_call" | custom-call | flops 294912 | bytes 983040 | tf_op jit(solution)/shard_map/pallas_call | solution.py:313
  75.3 7.7 %collective-permute-done.17.refs_2_ = bf16[512,128]{1,0:T(8,128)(2,1)S(1)} collective-permute-done((bf16[512,128]{1,0:T(8,128)(2,1)S(1)}, bf16[512,128]{1,0:T(8,128)(2,1)S(1)}, u32[]{:S(2)}, u32[]{:S(2)}) %collective-permute-start.17) | collective-permute-done | bytes 131104 | tf_op jit(solution)/shard_map/ppermute | solution.py:341
  83.0 0.9 %shard_map.126 = (bf16[128,2,128]{2,1,0:T(2,128)(2,1)}, bf16[128,2,128]{2,1,0:T(2,128)(2,1)}) custom-call(f32[512,128]{1,0:T(8,128)S(1)} %get-tuple-element.108.refs_0_, bf16[512,128]{1,0:T(8,128)(2,1)S(1)} %collective-permute-done.16.refs_1_, bf16[512,128]{1,0:T(8,128)(2,1)S(1)} %collective-permute-done.17.refs_2_, ...), custom_call_target="tpu_custom_call" | custom-call | flops 196608 | bytes 655360 | tf_op jit(solution)/shard_map/pallas_call | solution.py:313
  (16 shorter events, 0.1 us)
Async XLA Ops:
  2.7 10.9 %collective-permute-start.2 = (bf16[640,128]{1,0:T(8,128)(2,1)}, bf16[640,128]{1,0:T(8,128)(2,1)S(1)}, u32[]{:S(2)}, u32[]{:S(2)}) collective-permute-start(bf16[640,128]{1,0:T(8,128)(2,1)} %get-tuple-element.60.refs_0_), channel_id=1, source_target_pairs={{0,24},{8,16},{16,8},{24,0},{1,25},{9,17},{17,9},{25,1},{2,26},{10... | collective-permute-start | bytes 491528 | tf_op jit(solution)/shard_map/ppermute | solution.py:341
  7.8 14.1 %collective-permute-start.1 = (bf16[640,128]{1,0:T(8,128)(2,1)}, bf16[640,128]{1,0:T(8,128)(2,1)S(1)}, u32[]{:S(2)}, u32[]{:S(2)}) collective-permute-start(bf16[640,128]{1,0:T(8,128)(2,1)} %get-tuple-element.60.refs_0_), channel_id=1, source_target_pairs={{0,16},{8,24},{16,0},{24,8},{1,17},{9,25},{17,1},{25,9},{2,18},{10... | collective-permute-start | bytes 491528 | tf_op jit(solution)/shard_map/ppermute | solution.py:341
  7.8 14.1 %collective-permute-start = (bf16[640,128]{1,0:T(8,128)(2,1)}, bf16[640,128]{1,0:T(8,128)(2,1)S(1)}, u32[]{:S(2)}, u32[]{:S(2)}) collective-permute-start(bf16[640,128]{1,0:T(8,128)(2,1)} %get-tuple-element.60.refs_0_), channel_id=1, source_target_pairs={{0,8},{8,0},{16,24},{24,16},{1,9},{9,1},{17,25},{25,17},{2,10},{10... | collective-permute-start | bytes 491528 | tf_op jit(solution)/shard_map/ppermute | solution.py:341
  9.2 1.1 %copy-start = (bf16[1,192,16,128]{3,2,1,0:T(8,128)(2,1)S(1)}, bf16[1,192,16,128]{3,2,1,0:T(8,128)(2,1)}, u32[]{:S(2)}) copy-start(bf16[1,192,16,128]{3,2,1,0:T(8,128)(2,1)} %param.7) | copy-start | bytes 2359300
  10.3 1.1 %copy-start.1 = (bf16[1,192,16,128]{3,2,1,0:T(8,128)(2,1)S(1)}, bf16[1,192,16,128]{3,2,1,0:T(8,128)(2,1)}, u32[]{:S(2)}) copy-start(bf16[1,192,16,128]{3,2,1,0:T(8,128)(2,1)} %param.12) | copy-start | bytes 2359300
  11.4 0.9 %copy-start.2 = (bf16[640,128]{1,0:T(8,128)(2,1)S(1)}, bf16[640,128]{1,0:T(8,128)(2,1)}, u32[]{:S(2)}) copy-start(bf16[640,128]{1,0:T(8,128)(2,1)} %get-tuple-element.60.refs_0_) | copy-start | bytes 491524
  21.9 7.4 %collective-permute-start.3 = (bf16[1024,128]{1,0:T(8,128)(2,1)S(1)}, bf16[1024,128]{1,0:T(8,128)(2,1)S(1)}, u32[]{:S(2)}, u32[]{:S(2)}) collective-permute-start(bf16[1024,128]{1,0:T(8,128)(2,1)S(1)} %pad_maximum_fusion.refs_3_), channel_id=1, source_target_pairs={{0,4},{4,0},{1,5},{5,1},{2,6},{6,2},{3,7},{7,3},{8,12},{12,8},{9,1... | collective-permute-start | bytes 786440 | tf_op jit(solution)/shard_map/ppermute | solution.py:350
  23.5 14.7 %collective-permute-start.6 = (bf16[640,128]{1,0:T(8,128)(2,1)}, bf16[640,128]{1,0:T(8,128)(2,1)S(1)}, u32[]{:S(2)}, u32[]{:S(2)}) collective-permute-start(bf16[640,128]{1,0:T(8,128)(2,1)} %get-tuple-element.71.refs_1_), channel_id=1, source_target_pairs={{0,24},{8,16},{16,8},{24,0},{1,25},{9,17},{17,9},{25,1},{2,26},{10... | collective-permute-start | bytes 491528 | tf_op jit(solution)/shard_map/ppermute | solution.py:341
  26.0 12.8 %collective-permute-start.5 = (bf16[640,128]{1,0:T(8,128)(2,1)}, bf16[640,128]{1,0:T(8,128)(2,1)S(1)}, u32[]{:S(2)}, u32[]{:S(2)}) collective-permute-start(bf16[640,128]{1,0:T(8,128)(2,1)} %get-tuple-element.71.refs_1_), channel_id=1, source_target_pairs={{0,16},{8,24},{16,0},{24,8},{1,17},{9,25},{17,1},{25,9},{2,18},{10... | collective-permute-start | bytes 491528 | tf_op jit(solution)/shard_map/ppermute | solution.py:341
  26.0 12.8 %collective-permute-start.4 = (bf16[640,128]{1,0:T(8,128)(2,1)}, bf16[640,128]{1,0:T(8,128)(2,1)S(1)}, u32[]{:S(2)}, u32[]{:S(2)}) collective-permute-start(bf16[640,128]{1,0:T(8,128)(2,1)} %get-tuple-element.71.refs_1_), channel_id=1, source_target_pairs={{0,8},{8,0},{16,24},{24,16},{1,9},{9,1},{17,25},{25,17},{2,10},{10... | collective-permute-start | bytes 491528 | tf_op jit(solution)/shard_map/ppermute | solution.py:341
  38.8 8.5 %collective-permute-start.7 = (bf16[1024,128]{1,0:T(8,128)(2,1)S(1)}, bf16[1024,128]{1,0:T(8,128)(2,1)S(1)}, u32[]{:S(2)}, u32[]{:S(2)}) collective-permute-start(bf16[1024,128]{1,0:T(8,128)(2,1)S(1)} %pad_maximum_fusion.1.refs_3_), channel_id=1, source_target_pairs={{0,4},{4,0},{1,5},{5,1},{2,6},{6,2},{3,7},{7,3},{8,12},{12,8},{9,1... | collective-permute-start | bytes 786440 | tf_op jit(solution)/shard_map/ppermute | solution.py:350
  39.9 12.2 %collective-permute-start.8 = (bf16[384,128]{1,0:T(8,128)(2,1)S(1)}, bf16[384,128]{1,0:T(8,128)(2,1)S(1)}, u32[]{:S(2)}, u32[]{:S(2)}) collective-permute-start(bf16[384,128]{1,0:T(8,128)(2,1)S(1)} %get-tuple-element.79), channel_id=1, source_target_pairs={{8,0},{24,16},{9,1},{25,17},{10,2},{26,18},{11,3},{27,19},{12,4},{... | collective-permute-start | bytes 294920 | tf_op jit(solution)/shard_map/ppermute | solution.py:341
  41.2 11.8 %collective-permute-start.9 = (bf16[384,128]{1,0:T(8,128)(2,1)S(1)}, bf16[384,128]{1,0:T(8,128)(2,1)S(1)}, u32[]{:S(2)}, u32[]{:S(2)}) collective-permute-start(bf16[384,128]{1,0:T(8,128)(2,1)S(1)} %get-tuple-element.81), channel_id=1, source_target_pairs={{16,0},{24,8},{17,1},{25,9},{18,2},{26,10},{19,3},{27,11},{20,4},{... | collective-permute-start | bytes 294920 | tf_op jit(solution)/shard_map/ppermute | solution.py:341
  42.5 10.5 %collective-permute-start.10 = (bf16[384,128]{1,0:T(8,128)(2,1)S(1)}, bf16[384,128]{1,0:T(8,128)(2,1)S(1)}, u32[]{:S(2)}, u32[]{:S(2)}) collective-permute-start(bf16[384,128]{1,0:T(8,128)(2,1)S(1)} %get-tuple-element.83), channel_id=1, source_target_pairs={{24,0},{16,8},{25,1},{17,9},{26,2},{18,10},{27,3},{19,11},{28,4},{... | collective-permute-start | bytes 294920 | tf_op jit(solution)/shard_map/ppermute | solution.py:341
  44.0 19.6 %collective-permute-start.14 = (bf16[1024,128]{1,0:T(8,128)(2,1)S(1)}, bf16[1024,128]{1,0:T(8,128)(2,1)S(1)}, u32[]{:S(2)}, u32[]{:S(2)}) collective-permute-start(bf16[1024,128]{1,0:T(8,128)(2,1)S(1)} %get-tuple-element.106), channel_id=1, source_target_pairs={{0,4},{4,0},{1,5},{5,1},{2,6},{6,2},{3,7},{7,3},{8,12},{12,8},{9,1... | collective-permute-start | bytes 786440 | tf_op jit(solution)/shard_map/ppermute | solution.py:350
  57.9 6.4 %collective-permute-start.15 = (bf16[1024,128]{1,0:T(8,128)(2,1)S(1)}, bf16[1024,128]{1,0:T(8,128)(2,1)S(1)}, u32[]{:S(2)}, u32[]{:S(2)}) collective-permute-start(bf16[1024,128]{1,0:T(8,128)(2,1)S(1)} %get-tuple-element.107), channel_id=1, source_target_pairs={{0,4},{4,0},{1,5},{5,1},{2,6},{6,2},{3,7},{7,3},{8,12},{12,8},{9,1... | collective-permute-start | bytes 786440 | tf_op jit(solution)/shard_map/ppermute | solution.py:350
  59.4 10.5 %collective-permute-start.11 = (bf16[384,128]{1,0:T(8,128)(2,1)S(1)}, bf16[384,128]{1,0:T(8,128)(2,1)S(1)}, u32[]{:S(2)}, u32[]{:S(2)}) collective-permute-start(bf16[384,128]{1,0:T(8,128)(2,1)S(1)} %get-tuple-element.99), channel_id=1, source_target_pairs={{8,0},{24,16},{9,1},{25,17},{10,2},{26,18},{11,3},{27,19},{12,4},{... | collective-permute-start | bytes 294920 | tf_op jit(solution)/shard_map/ppermute | solution.py:341
  60.7 13.6 %collective-permute-start.12 = (bf16[384,128]{1,0:T(8,128)(2,1)S(1)}, bf16[384,128]{1,0:T(8,128)(2,1)S(1)}, u32[]{:S(2)}, u32[]{:S(2)}) collective-permute-start(bf16[384,128]{1,0:T(8,128)(2,1)S(1)} %get-tuple-element.100), channel_id=1, source_target_pairs={{16,0},{24,8},{17,1},{25,9},{18,2},{26,10},{19,3},{27,11},{20,4},{... | collective-permute-start | bytes 294920 | tf_op jit(solution)/shard_map/ppermute | solution.py:341
  62.0 12.3 %collective-permute-start.13 = (bf16[384,128]{1,0:T(8,128)(2,1)S(1)}, bf16[384,128]{1,0:T(8,128)(2,1)S(1)}, u32[]{:S(2)}, u32[]{:S(2)}) collective-permute-start(bf16[384,128]{1,0:T(8,128)(2,1)S(1)} %get-tuple-element.101), channel_id=1, source_target_pairs={{24,0},{16,8},{25,1},{17,9},{26,2},{18,10},{27,3},{19,11},{28,4},{... | collective-permute-start | bytes 294920 | tf_op jit(solution)/shard_map/ppermute | solution.py:341
  64.4 10.9 %collective-permute-start.16 = (bf16[512,128]{1,0:T(8,128)(2,1)S(1)}, bf16[512,128]{1,0:T(8,128)(2,1)S(1)}, u32[]{:S(2)}, u32[]{:S(2)}) collective-permute-start(bf16[512,128]{1,0:T(8,128)(2,1)S(1)} %get-tuple-element.109), channel_id=1, source_target_pairs={{8,0},{0,8},{24,16},{16,24},{9,1},{1,9},{25,17},{17,25},{10,2},{2,... | collective-permute-start | bytes 393224 | tf_op jit(solution)/shard_map/ppermute | solution.py:341
  66.6 16.4 %collective-permute-start.17 = (bf16[512,128]{1,0:T(8,128)(2,1)S(1)}, bf16[512,128]{1,0:T(8,128)(2,1)S(1)}, u32[]{:S(2)}, u32[]{:S(2)}) collective-permute-start(bf16[512,128]{1,0:T(8,128)(2,1)S(1)} %get-tuple-element.110), channel_id=1, source_target_pairs={{16,0},{24,8},{0,16},{8,24},{17,1},{25,9},{1,17},{9,25},{18,2},{26... | collective-permute-start | bytes 393224 | tf_op jit(solution)/shard_map/ppermute | solution.py:341
  69.9 13.1 %collective-permute-start.18 = (bf16[512,128]{1,0:T(8,128)(2,1)S(1)}, bf16[512,128]{1,0:T(8,128)(2,1)S(1)}, u32[]{:S(2)}, u32[]{:S(2)}) collective-permute-start(bf16[512,128]{1,0:T(8,128)(2,1)S(1)} %get-tuple-element.111), channel_id=1, source_target_pairs={{24,0},{16,8},{8,16},{0,24},{25,1},{17,9},{9,17},{1,25},{26,2},{18... | collective-permute-start | bytes 393224 | tf_op jit(solution)/shard_map/ppermute | solution.py:341

commit v2 on v1

--- a/solution.py
+++ b/solution.py
@@ -95,7 +95,7 @@
     return outs[:groups], outs[groups : 2 * groups], outs[2 * groups :]
 
 
-def attend(scalars, queries, cotangent, prompts, rollouts, roll_size, block, first, end, carry):
+def attend(scalars, queries, cotangent, prompts, rollouts, roll_size, bundles, block, first, end, carry):
     flat, dim = queries.shape
     seq_size = len(rollouts)
     prow, rrow = prompts[0][2] // 2, rollouts[0][2] // 2
@@ -124,7 +124,7 @@
         else:
             k_s, v_s = source_refs[:2]
         if closing:
-            line_refs, grad_refs = rest[:roll_size], rest[roll_size : roll_size + seq_size]
+            line_refs, grad_refs = rest[:roll_size], rest[roll_size : roll_size + len(bundles)]
         dk_s, dv_s = rest[-2:]
         live = scalar_ref[0]
         rank = scalar_ref[1]
@@ -197,10 +197,11 @@
                 at = 2 * slot * prow
                 ref[at : at + prow, :] = dk[lower : lower + prow, :].astype(ref.dtype)
                 ref[at + prow : at + 2 * prow, :] = dv[lower : lower + prow, :].astype(ref.dtype)
-        for slot, ref in enumerate(grad_refs):
-            lower = prompt_total + slot * rrow
-            ref[:rrow, :] = dk[lower : lower + rrow, :].astype(ref.dtype)
-            ref[rrow:, :] = dv[lower : lower + rrow, :].astype(ref.dtype)
+        for (members, _), ref in zip(bundles, grad_refs):
+            for i, slot in enumerate(members):
+                lower, at = prompt_total + slot * rrow, 2 * i * rrow
+                ref[at : at + rrow, :] = dk[lower : lower + rrow, :].astype(ref.dtype)
+                ref[at + rrow : at + 2 * rrow, :] = dv[lower : lower + rrow, :].astype(ref.dtype)
 
     shapes = [((here, dim), BF16), ((here, total), BF16)]
     sums = [((dim, total), F32)] * 2
@@ -208,7 +209,7 @@
         shapes += [((total, dim), BF16)] * 2
     if closing:
         shapes += [((seq_size * 2 * prow, dim), BF16 if dx else F32) for dx in range(roll_size)]
-        shapes += [((2 * rrow, dim), BF16 if slot else F32) for slot in range(seq_size)]
+        shapes += [((2 * rrow * len(members), dim), kind) for members, kind in bundles]
     else:
         shapes += sums
     outs = pl.pallas_call(
@@ -222,7 +223,7 @@
     )(scalars, queries, cotangent, *sources)
     part, rest = tuple(outs[:2]), list(outs[2:])
     if not closing:
-        return part, rest
+        return part, rest if opening else list(carry[:2]) + rest
     keys, rest = (rest[0], rest[2:]) if opening else (carry[0], rest)
     return part, keys, rest[:roll_size], rest[roll_size:]
 
@@ -264,30 +265,51 @@
     )(*arrays, *keys)
 
 
-def pair_sum(owns, received, seq_size):
-    groups = len(owns)
-    rows, dim = owns[0].shape
+def pair_sum(own, received, bundles, seq_size):
+    rows, dim = own.shape
     part = rows // seq_size
-    count = len(received[0])
+    count = len(received)
+
+    def body(own_ref, *refs):
+        others, outs = refs[:count], refs[count:]
+        for (members, _), out in zip(bundles, outs):
+            for i, slot in enumerate(members):
+                span = slice(slot * part, (slot + 1) * part)
+                value = own_ref[span, :]
+                for other in others:
+                    value = value + other[span, :].astype(F32)
+                out[i * part : (i + 1) * part, :] = value.astype(out.dtype)
+
+    return pl.pallas_call(
+        body,
+        out_shape=[jax.ShapeDtypeStruct((part * len(members), dim), kind) for members, kind in bundles],
+        in_specs=[VMEM] * (1 + count),
+        out_specs=[VMEM] * len(bundles),
+        compiler_params=params(),
+        cost_estimate=cost(rows * dim, rows * dim * 10),
+    )(own, *received)
+
+
+def fold(bundled, received):
+    count = len(bundled)
+    rows, dim = bundled[0][0].shape
 
     def body(*refs):
-        own_refs, other_refs, outs = refs[:groups], refs[groups : groups * (1 + count)], refs[groups * (1 + count) :]
-        for slot, out in enumerate(outs):
-            span = slice(slot * part, (slot + 1) * part)
-            for g, own_ref in enumerate(own_refs):
-                value = own_ref[span, :]
-                for other in other_refs[g * count : (g + 1) * count]:
-                    value = value + other[span, :].astype(F32)
-                out[g * part : (g + 1) * part, :] = value.astype(out.dtype)
+        owns, theirs, came = refs[:count], refs[count : 2 * count], refs[2 * count : 3 * count]
+        kept_ref, sent_ref = refs[3 * count :]
+        for i in range(count):
+            span = slice(i * rows, (i + 1) * rows)
+            kept_ref[span, :] = owns[i][...] + came[i][:rows, :].astype(F32)
+            sent_ref[span, :] = (theirs[i][...] + came[i][rows:, :].astype(F32)).astype(BF16)
 
     return pl.pallas_call(
         body,
-        out_shape=[jax.ShapeDtypeStruct((groups * part, dim), BF16 if slot else F32) for slot in range(seq_size)],
-        in_specs=[VMEM] * (groups * (1 + count)),
-        out_specs=[VMEM] * seq_size,
-        compiler_params=params(),
-        cost_estimate=cost(groups * rows * dim, groups * rows * dim * 10),
-    )(*owns, *[item for line in received for item in line])
+        out_shape=[jax.ShapeDtypeStruct((count * rows, dim), kind) for kind in (F32, BF16)],
+        in_specs=[VMEM] * (3 * count),
+        out_specs=[VMEM] * 2,
+        compiler_params=params(),
+        cost_estimate=cost(2 * count * rows * dim, count * rows * dim * 18),
+    )(*[item[0] for item in bundled], *[item[2] for item in bundled], *received)
 
 
 def finish(owns, received, groups):
@@ -340,11 +362,24 @@
     def over_seq(value, which):
         return lax.ppermute(value, "seq", which)
 
-    def give_back(value, slot):
-        return over_seq(value, [(b, a) for a, b in pairs(slot)])
-
-    def give_down(value, slot):
-        return over_seq(value, [(b, a) for a, b in pairs(slot) if a < b])
+    halving = seq_size == 4
+    if halving:
+        bundles = [((0,), F32), ((1, 3), BF16), ((2,), F32)]
+    else:
+        bundles = [((0,), F32)] + [((slot,), BF16) for slot in slots]
+
+    def give(bundled, down):
+        came = []
+        for (members, kind), value in zip(bundles, bundled):
+            if kind == BF16:
+                back = [(b, a) for a, b in pairs(members[0])]
+                if down:
+                    back = [(a, b) for a, b in back if b < a or (len(members) > 1 and a ^ members[1] < a)]
+                came.append(over_seq(value, back))
+        return came
+
+    def give_far(value, down):
+        return over_seq(value, [(a, b) for a, b in pairs(2) if b < a or not down])
 
     def over_roll(value, shift):
         return lax.ppermute(value, "roll", [(i, (i + shift) % roll_size) for i in range(roll_size)])
@@ -364,38 +399,66 @@
     lines = send_over_roll(messages)
     block = math.gcd(flat, 256)
     steps = flat // block
-    heads, all_keys, line_own, line_got, roll_own, roll_got = [], [], [], [], [], []
+    heads, all_keys, prompt_sums, prompt_came, row_sums, row_came = [], [], [], [], [], []
+
+    def settle_rows(sums, came):
+        if halving:
+            mine, sent = fold([sums], came)
+            row_sums.append(mine)
+            row_came.append([give_far(sent, True)])
+        else:
+            row_sums.append(sums[0])
+            row_came.append(came)
+
+    def settle_prompt(line_grads, came):
+        prompt_sums.append(pair_sum(line_grads[0], came, bundles, seq_size))
+        prompt_came.append(give(prompt_sums[-1], False))
+
+    def back_over_roll(line_grads):
+        return [over_roll(line_grads[shift], -shift) for shift in range(1, roll_size)]
+
+    waiting = None
     for g in range(groups):
         prompts = [(item, slot * prows, prows) for item in lines for slot in range(seq_size)]
         rollouts = [(item, prows, rrows) for item in messages]
         if g + 1 < groups:
             messages = send_over_seq(after(own[g + 1], lines[0]), kept[g + 1])
-        cuts = [0, steps // 2, steps] if g else [0, steps]
+        cuts = sorted({0, 1, steps - 1, steps}) if g else [0, steps]
         parts, carry = [], []
         for start, stop in zip(cuts, cuts[1:]):
-            if start:
-                carry = [after(item, roll_got[g - 1]) for item in carry]
+            if waiting and start:
+                sums, came, line_grads = waiting
+                settle_rows(sums, [after(item, parts) for item in came])
+                line_grads = [after(item, parts) for item in line_grads]
+                line_came = back_over_roll(line_grads)
+                waiting = None
+            elif start:
+                carry = [after(item, row_came[-1], line_came) for item in carry]
             part, *rest = attend(
-                scalars, q_groups[g], cot_groups[g], prompts, rollouts, roll_size, block, start, stop, carry
+                scalars, q_groups[g], cot_groups[g], prompts, rollouts, roll_size, bundles, block, start, stop, carry
             )
             parts.append(part)
             carry = rest[0]
+        if g:
+            settle_prompt(line_grads, line_came)
         keys, line_grads, roll_grads = rest
         heads.append(parts)
         all_keys.append(keys)
-        line_own.append(line_grads[0])
-        line_got.append([over_roll(line_grads[shift], -shift) for shift in range(1, roll_size)])
         if g + 1 < groups:
             messages = [after(item, parts) for item in messages]
             lines = send_over_roll(messages)
             roll_grads = [after(item, lines[0]) for item in roll_grads]
-        roll_own.append(roll_grads[0])
-        roll_got.append([give_down(roll_grads[slot], slot) for slot in slots])
-
-    sums = pair_sum(line_own, line_got, seq_size)
+        waiting = (roll_grads, give(roll_grads, True), line_grads)
+    settle_rows(*waiting[:2])
+    settle_prompt(line_grads, back_over_roll(line_grads))
+
     attention_rows, grad_rows = row_outputs(heads, all_keys, row_count, block)
-    grad_rk, grad_rv = finish(roll_own, roll_got, groups)
-    grad_pk, grad_pv = finish([sums[0]], [[give_back(sums[slot], slot) for slot in slots]], groups)
+    grad_rk, grad_rv = finish(row_sums, row_came, groups)
+    if halving:
+        summed, sent = fold(prompt_sums, [came[0] for came in prompt_came])
+        grad_pk, grad_pv = finish([summed], [[give_far(sent, False)]], groups)
+    else:
+        grad_pk, grad_pv = finish([sums[0] for sums in prompt_sums], prompt_came, groups)
     return attention_rows[None], grad_rows[None], grad_rk[None], grad_rv[None], grad_pk, grad_pv
 
 

time: 84.3 us -> 84.5 us (level)
  starting transfers between devices: 29 us -> 27.3 us
  waiting for transfers between devices: 21.9 us -> 23 us
    ppermute x4, waiting for transfers between devices: 4.48 us -> 7.24 us  [over_roll(): lax.ppermute(value, 'roll', [(i, (i + shift) % roll_size) for i in range(...]
    ppermute x15 -> x13, waiting for transfers between devices: 17.4 us -> 15.8 us  [over_seq(): return lax.ppermute(value, 'seq', which)]
    ppermute x15 -> x13, starting transfers between devices: 23.8 us -> 22.5 us  [over_seq(): return lax.ppermute(value, 'seq', which)]
    pallas_call x3 -> x4, Pallas kernels: 18.6 us -> 19.4 us  [attend(): pl.pallas_call(body, out_shape=[jax.ShapeDtypeStruct(shape, kind) for sha...]
  transfers between devices with their start and end apart: 19 -> 17, of which waited for: 8 -> 8; matrix products, arithmetic and copies ran while one was open for 0% -> 0% of each run, Pallas kernels for 30% -> 28%
where the time goes in v2:
time: 84.5 us; the launch traced here: 84.2 us
  Pallas kernels  29 us (34%)
  starting transfers between devices  27.3 us (32%)
  waiting for transfers between devices  23 us (27%)
  local copies, waits for them, and re-layouts  3.31 us (4%)
  between operations  1.51 us (2%)
    ppermute x13, starting transfers between devices, over_seq(): return lax.ppermute(value, 'seq', which)  22.5 us
    pallas_call x4, Pallas kernels, attend(): pl.pallas_call(body, out_shape=[jax.ShapeDtypeStruct(shape, kind) for sha...  19.4 us
    ppermute x13, waiting for transfers between devices, over_seq(): return lax.ppermute(value, 'seq', which)  15.8 us
    ppermute x4, waiting for transfers between devices, over_roll(): lax.ppermute(value, 'roll', [(i, (i + shift) % roll_size) for i in range(...  7.24 us
    ppermute x4, starting transfers between devices, over_roll(): lax.ppermute(value, 'roll', [(i, (i + shift) % roll_size) for i in range(...  4.79 us
    pallas_call x1, Pallas kernels, row_outputs(): pl.pallas_call(body, out_shape=[jax.ShapeDtypeStruct((rows, per * groups,...  4.24 us
    unnamed x6, local copies, waits for them, and re-layouts  3.18 us
    pallas_call x1, Pallas kernels, split_heads(): pl.pallas_call(body, out_shape=[jax.ShapeDtypeStruct((starts[-1], dim), B...  2.03 us
  transfers between devices with their start and end apart: 17, of which 8 were waited for; matrix products, arithmetic and copies ran while one was open for 0% of the time, Pallas kernels for 28%

profile of v2, /device:TPU:0, one launch (start us, length us, event | category | flops | bytes accessed | tf_op | source)
XLA Modules:
  0.0 84.2 jit_solution(3633367025408936832)
XLA Ops:
  0.6 2.0 %shard_map.118 = (bf16[640,128]{1,0:T(8,128)(2,1)}, bf16[640,128]{1,0:T(8,128)(2,1)}) custom-call(bf16[128,2,128]{2,1,0:T(2,128)(2,1)} %refs_0_.1, bf16[128,2,128]{2,1,0:T(2,128)(2,1)} %refs_1_.1, bf16[192,2,128]{2,1,0:T(2,128)(2,1)} %bitcast.17, bf16[192,2,128]{2,1,0:T(2,128)(2,1)} %bitcast.18), custom_call_target="tpu_custom_call" | custom-call | bytes 1310720 | tf_op jit(solution)/shard_map/pallas_call | solution.py:57
  2.7 5.1 %collective-permute-start.2 = (bf16[640,128]{1,0:T(8,128)(2,1)}, bf16[640,128]{1,0:T(8,128)(2,1)S(1)}, u32[]{:S(2)}, u32[]{:S(2)}) collective-permute-start(bf16[640,128]{1,0:T(8,128)(2,1)} %get-tuple-element.72.refs_0_), channel_id=1, source_target_pairs={{0,24},{8,16},{16,8},{24,0},{1,25},{9,17},{17,9},{25,1},{2,26},{10... | collective-permute-start | bytes 491528 | tf_op jit(solution)/shard_map/ppermute | solution.py:363
  7.8 0.0 collective-permute-start.1
  7.8 0.6 collective-permute-start
  9.1 0.1 stack.23.scalar_ref.refs_0_
  9.2 1.1 %copy-done = bf16[1,192,16,128]{3,2,1,0:T(8,128)(2,1)S(1)} copy-done((bf16[1,192,16,128]{3,2,1,0:T(8,128)(2,1)S(1)}, bf16[1,192,16,128]{3,2,1,0:T(8,128)(2,1)}, u32[]{:S(2)}) %copy-start) | copy-done | bytes 786456
  10.3 1.1 %copy-done.1 = bf16[1,192,16,128]{3,2,1,0:T(8,128)(2,1)S(1)} copy-done((bf16[1,192,16,128]{3,2,1,0:T(8,128)(2,1)S(1)}, bf16[1,192,16,128]{3,2,1,0:T(8,128)(2,1)}, u32[]{:S(2)}) %copy-start.1) | copy-done | bytes 786456
  11.4 0.9 %copy-done.2 = bf16[640,128]{1,0:T(8,128)(2,1)S(1)} copy-done((bf16[640,128]{1,0:T(8,128)(2,1)S(1)}, bf16[640,128]{1,0:T(8,128)(2,1)}, u32[]{:S(2)}) %copy-start.2) | copy-done | bytes 163864
  12.3 1.2 %shard_map.119 = (bf16[1536,128]{1,0:T(8,128)(2,1)S(1)}, bf16[1536,128]{1,0:T(8,128)(2,1)S(1)}, bf16[1536,128]{1,0:T(8,128)(2,1)S(1)}, bf16[1536,128]{1,0:T(8,12...) custom-call(s32[5]{0:T(128)S(1)} %stack.23.scalar_ref.refs_0_, ...), custom_call_target="tpu_custom_call" | custom-call | bytes 6291456 | tf_op jit(solution)/shard_map/pallas_call | solution.py:87
  13.6 0.0 collective-permute-done.2.refs_8_
  13.6 8.2 %collective-permute-done.1.refs_7_ = bf16[640,128]{1,0:T(8,128)(2,1)S(1)} collective-permute-done((bf16[640,128]{1,0:T(8,128)(2,1)}, bf16[640,128]{1,0:T(8,128)(2,1)S(1)}, u32[]{:S(2)}, u32[]{:S(2)}) %collective-permute-start.1) | collective-permute-done | bytes 163872 | tf_op jit(solution)/shard_map/ppermute | solution.py:363
  21.9 0.0 collective-permute-done.refs_6_
  21.9 1.6 %collective-permute-start.3 = (bf16[1024,128]{1,0:T(8,128)(2,1)S(1)}, bf16[1024,128]{1,0:T(8,128)(2,1)S(1)}, u32[]{:S(2)}, u32[]{:S(2)}) collective-permute-start(bf16[1024,128]{1,0:T(8,128)(2,1)S(1)} %pad_maximum_fusion.refs_3_), channel_id=1, source_target_pairs={{0,4},{4,0},{1,5},{5,1},{2,6},{6,2},{3,7},{7,3},{8,12},{12,8},{9,1... | collective-permute-start | bytes 786440 | tf_op jit(solution)/shard_map/ppermute | solution.py:385
  23.5 2.5 %collective-permute-start.6 = (bf16[640,128]{1,0:T(8,128)(2,1)}, bf16[640,128]{1,0:T(8,128)(2,1)S(1)}, u32[]{:S(2)}, u32[]{:S(2)}) collective-permute-start(bf16[640,128]{1,0:T(8,128)(2,1)} %get-tuple-element.83.refs_1_), channel_id=1, source_target_pairs={{0,24},{8,16},{16,8},{24,0},{1,25},{9,17},{17,9},{25,1},{2,26},{10... | collective-permute-start | bytes 491528 | tf_op jit(solution)/shard_map/ppermute | solution.py:363
  26.0 0.0 collective-permute-start.5
  26.0 1.9 %collective-permute-start.4 = (bf16[640,128]{1,0:T(8,128)(2,1)}, bf16[640,128]{1,0:T(8,128)(2,1)S(1)}, u32[]{:S(2)}, u32[]{:S(2)}) collective-permute-start(bf16[640,128]{1,0:T(8,128)(2,1)} %get-tuple-element.83.refs_1_), channel_id=1, source_target_pairs={{0,8},{8,0},{16,24},{24,16},{1,9},{9,1},{17,25},{25,17},{2,10},{10... | collective-permute-start | bytes 491528 | tf_op jit(solution)/shard_map/ppermute | solution.py:363
  27.9 1.5 %collective-permute-done.3.refs_4_ = bf16[1024,128]{1,0:T(8,128)(2,1)S(1)} collective-permute-done((bf16[1024,128]{1,0:T(8,128)(2,1)S(1)}, bf16[1024,128]{1,0:T(8,128)(2,1)S(1)}, u32[]{:S(2)}, u32[]{:S(2)}) %collective-permute-start.3) | collective-permute-done | bytes 262176 | tf_op jit(solution)/shard_map/ppermute | solution.py:385
  29.4 8.9 %shard_map.120 = (bf16[1536,128]{1,0:T(8,128)(2,1)S(1)}, bf16[1536,1792]{1,0:T(8,128)(2,1)S(1)}, bf16[1792,128]{1,0:T(8,128)(2,1)S(1)}, bf16[1792,128]{1,0:T(8,1...) custom-call(s32[5]{0:T(128)S(1)} %stack.23.scalar_ref.refs_0_, ...), custom_call_target="tpu_custom_call" | custom-call | flops 7046430720 | bytes 3145728 | tf_op jit(solution)/shard_map/pallas_call | solution.py:215
  38.2 0.0 collective-permute-done.6.refs_8_
  38.2 0.5 collective-permute-done.5.refs_7_
  38.7 0.0 collective-permute-done.4.refs_6_
  38.8 1.1 %collective-permute-start.7 = (bf16[1024,128]{1,0:T(8,128)(2,1)S(1)}, bf16[1024,128]{1,0:T(8,128)(2,1)S(1)}, u32[]{:S(2)}, u32[]{:S(2)}) collective-permute-start(bf16[1024,128]{1,0:T(8,128)(2,1)S(1)} %pad_maximum_fusion.1.refs_3_), channel_id=1, source_target_pairs={{0,4},{4,0},{1,5},{5,1},{2,6},{6,2},{3,7},{7,3},{8,12},{12,8},{9,1... | collective-permute-start | bytes 786440 | tf_op jit(solution)/shard_map/ppermute | solution.py:385
  39.9 1.3 %collective-permute-start.8 = (bf16[768,128]{1,0:T(8,128)(2,1)S(1)}, bf16[768,128]{1,0:T(8,128)(2,1)S(1)}, u32[]{:S(2)}, u32[]{:S(2)}) collective-permute-start(bf16[768,128]{1,0:T(8,128)(2,1)S(1)} %get-tuple-element.100), channel_id=1, source_target_pairs={{8,0},{24,16},{16,24},{9,1},{25,17},{17,25},{10,2},{26,18},{18,26}... | collective-permute-start | bytes 589832 | tf_op jit(solution)/shard_map/ppermute | solution.py:363
  41.2 4.9 %collective-permute-done.7.refs_4_ = bf16[1024,128]{1,0:T(8,128)(2,1)S(1)} collective-permute-done((bf16[1024,128]{1,0:T(8,128)(2,1)S(1)}, bf16[1024,128]{1,0:T(8,128)(2,1)S(1)}, u32[]{:S(2)}, u32[]{:S(2)}) %collective-permute-start.7) | collective-permute-done | bytes 262176 | tf_op jit(solution)/shard_map/ppermute | solution.py:385
  46.1 2.2 %shard_map.121 = (bf16[256,128]{1,0:T(8,128)(2,1)S(1)}, bf16[256,1792]{1,0:T(8,128)(2,1)S(1)}, bf16[1792,128]{1,0:T(8,128)(2,1)S(1)}, bf16[1792,128]{1,0:T(8,128...) custom-call(s32[5]{0:T(128)S(1)} %stack.23.scalar_ref.refs_0_, ...), custom_call_target="tpu_custom_call" | custom-call | flops 1174405120 | bytes 524288 | tf_op jit(solution)/shard_map/pallas_call | solution.py:215
  48.3 0.0 collective-permute-done.8.refs_2_
  48.4 1.5 %collective-permute-start.9 = (bf16[384,128]{1,0:T(8,128)(2,1)S(1)}, bf16[384,128]{1,0:T(8,128)(2,1)S(1)}, u32[]{:S(2)}, u32[]{:S(2)}) collective-permute-start(bf16[384,128]{1,0:T(8,128)(2,1)S(1)} %get-tuple-element.102), channel_id=1, source_target_pairs={{16,0},{24,8},{17,1},{25,9},{18,2},{26,10},{19,3},{27,11},{20,4},{... | collective-permute-start | bytes 294920 | tf_op jit(solution)/shard_map/ppermute | solution.py:363
  49.9 0.6 collective-permute-start.10
  50.5 6.0 %shard_map.122 = (bf16[1024,128]{1,0:T(8,128)(2,1)S(1)}, bf16[1024,1792]{1,0:T(8,128)(2,1)S(1)}, f32[128,1792]{1,0:T(8,128)S(1)}, f32[128,1792]{1,0:T(8,128)S(1)}) custom-call(s32[5]{0:T(128)S(1)} %stack.23.scalar_ref.refs_0_, bf16[1536,128]{1,0:T(8,128)(2,1)S(1)} %get-tuple-element.79.refs_1_, bf16[1536,128]{1,0:T(8,128)(2,1)S(1)} %get-tuple-element.80.refs_2_, ...), custom_call_target="tpu_custom_call" | custom-call | flops 4697620480 | bytes 2097152 | tf_op jit(solution)/shard_map/pallas_call | solution.py:215
  56.5 0.0 collective-permute-done.9.refs_2_
  56.5 0.0 collective-permute-done.10.refs_0_
  56.5 2.3 %shard_map.124 = (bf16[256,128]{1,0:T(8,128)(2,1)S(1)}, bf16[256,1792]{1,0:T(8,128)(2,1)S(1)}, f32[1024,128]{1,0:T(8,128)S(1)}, bf16[1024,128]{1,0:T(8,128)(2,1)...) custom-call(s32[5]{0:T(128)S(1)} %stack.23.scalar_ref.refs_0_, ...), custom_call_target="tpu_custom_call" | custom-call | flops 1174405120 | bytes 524288 | tf_op jit(solution)/shard_map/pallas_call | solution.py:215
  58.8 1.6 %collective-permute-start.13 = (bf16[1024,128]{1,0:T(8,128)(2,1)S(1)}, bf16[1024,128]{1,0:T(8,128)(2,1)S(1)}, u32[]{:S(2)}, u32[]{:S(2)}) collective-permute-start(bf16[1024,128]{1,0:T(8,128)(2,1)S(1)} %get-tuple-element.128), channel_id=1, source_target_pairs={{0,4},{4,0},{1,5},{5,1},{2,6},{6,2},{3,7},{7,3},{8,12},{12,8},{9,1... | collective-permute-start | bytes 786440 | tf_op jit(solution)/shard_map/ppermute | solution.py:385
  60.4 1.3 %collective-permute-start.11 = (bf16[768,128]{1,0:T(8,128)(2,1)S(1)}, bf16[768,128]{1,0:T(8,128)(2,1)S(1)}, u32[]{:S(2)}, u32[]{:S(2)}) collective-permute-start(bf16[768,128]{1,0:T(8,128)(2,1)S(1)} %get-tuple-element.119), channel_id=1, source_target_pairs={{8,0},{24,16},{16,24},{9,1},{25,17},{17,25},{10,2},{26,18},{18,26}... | collective-permute-start | bytes 589832 | tf_op jit(solution)/shard_map/ppermute | solution.py:363
  61.7 2.7 %collective-permute-start.14 = (bf16[512,128]{1,0:T(8,128)(2,1)S(1)}, bf16[512,128]{1,0:T(8,128)(2,1)S(1)}, u32[]{:S(2)}, u32[]{:S(2)}) collective-permute-start(bf16[512,128]{1,0:T(8,128)(2,1)S(1)} %get-tuple-element.132), channel_id=1, source_target_pairs={{8,0},{0,8},{24,16},{16,24},{9,1},{1,9},{25,17},{17,25},{10,2},{2,... | collective-permute-start | bytes 393224 | tf_op jit(solution)/shard_map/ppermute | solution.py:363
  64.5 0.8 collective-permute-done.13.refs_0_
  65.3 0.1 collective-permute-start.15
  65.4 4.0 %collective-permute-done.11.refs_2_ = bf16[768,128]{1,0:T(8,128)(2,1)S(1)} collective-permute-done((bf16[768,128]{1,0:T(8,128)(2,1)S(1)}, bf16[768,128]{1,0:T(8,128)(2,1)S(1)}, u32[]{:S(2)}, u32[]{:S(2)}) %collective-permute-start.11) | collective-permute-done | bytes 196640 | tf_op jit(solution)/shard_map/ppermute | solution.py:363
  69.5 1.3 %collective-permute-start.12 = (bf16[384,128]{1,0:T(8,128)(2,1)S(1)}, bf16[384,128]{1,0:T(8,128)(2,1)S(1)}, u32[]{:S(2)}, u32[]{:S(2)}) collective-permute-start(bf16[384,128]{1,0:T(8,128)(2,1)S(1)} %get-tuple-element.121), channel_id=1, source_target_pairs={{16,0},{24,8},{17,1},{25,9},{18,2},{26,10},{19,3},{27,11},{20,4},{... | collective-permute-start | bytes 294920 | tf_op jit(solution)/shard_map/ppermute | solution.py:363
  70.8 1.1 %collective-permute-done.14.refs_4_ = bf16[512,128]{1,0:T(8,128)(2,1)S(1)} collective-permute-done((bf16[512,128]{1,0:T(8,128)(2,1)S(1)}, bf16[512,128]{1,0:T(8,128)(2,1)S(1)}, u32[]{:S(2)}, u32[]{:S(2)}) %collective-permute-start.14) | collective-permute-done | bytes 131104 | tf_op jit(solution)/shard_map/ppermute | solution.py:363
  71.9 1.9 %collective-permute-done.15.refs_5_ = bf16[512,128]{1,0:T(8,128)(2,1)S(1)} collective-permute-done((bf16[512,128]{1,0:T(8,128)(2,1)S(1)}, bf16[512,128]{1,0:T(8,128)(2,1)S(1)}, u32[]{:S(2)}, u32[]{:S(2)}) %collective-permute-start.15) | collective-permute-done | bytes 131104 | tf_op jit(solution)/shard_map/ppermute | solution.py:363
  73.8 0.1 shard_map.130
  73.8 4.2 %collective-permute-start.16 = (bf16[512,128]{1,0:T(8,128)(2,1)S(1)}, bf16[512,128]{1,0:T(8,128)(2,1)S(1)}, u32[]{:S(2)}, u32[]{:S(2)}) collective-permute-start(bf16[512,128]{1,0:T(8,128)(2,1)S(1)} %get-tuple-element.135), channel_id=1, source_target_pairs={{0,16},{8,24},{16,0},{24,8},{1,17},{9,25},{17,1},{25,9},{2,18},{10... | collective-permute-start | bytes 393224 | tf_op jit(solution)/shard_map/ppermute | solution.py:363
  78.1 4.2 %shard_map.125 = (bf16[192,16,128]{2,1,0:T(8,128)(2,1)}, bf16[192,16,128]{2,1,0:T(8,128)(2,1)}) custom-call(bf16[1536,128]{1,0:T(8,128)(2,1)S(1)} %get-tuple-element.77.refs_0_, bf16[1536,1792]{1,0:T(8,128)(2,1)S(1)} %get-tuple-element.78.refs_1_, bf16[256,128]{1,0:T(8,128)(2,1)S(1)} %get-tuple-element.87.refs_2_, ...), custom_call_target="tpu_custom_call" | custom-call | flops 2818572288 | bytes 11010048 | tf_op jit(solution)/shard_map/pallas_call | solution.py:258
  82.3 0.0 collective-permute-done.12.refs_3_
  82.3 1.0 %shard_map.127 = (bf16[192,2,128]{2,1,0:T(2,128)(2,1)}, bf16[192,2,128]{2,1,0:T(2,128)(2,1)}) custom-call(f32[384,128]{1,0:T(8,128)S(1)} %get-tuple-element.116.refs_0_, f32[384,128]{1,0:T(8,128)S(1)} %get-tuple-element.120.refs_1_, bf16[384,128]{1,0:T(8,128)(2,1)S(1)} %collective-permute-done.9.refs_2_, bf16[384,128]{1,0:T(8,128)(2,1)S(1)} %collective-permute-done.12.refs_3_), custom_call_target="tpu_custom_call" | custom-call | flops 98304 | bytes 983040 | tf_op jit(solution)/shard_map/pallas_call | solution.py:335
  83.3 0.0 collective-permute-done.16.refs_1_
  83.3 0.9 %shard_map.131 = (bf16[128,2,128]{2,1,0:T(2,128)(2,1)}, bf16[128,2,128]{2,1,0:T(2,128)(2,1)}) custom-call(f32[512,128]{1,0:T(8,128)S(1)} %get-tuple-element.134.refs_0_, bf16[512,128]{1,0:T(8,128)(2,1)S(1)} %collective-permute-done.16.refs_1_), custom_call_target="tpu_custom_call" | custom-call | flops 65536 | bytes 655360 | tf_op jit(solution)/shard_map/pallas_call | solution.py:335
  (17 shorter events, 0.3 us)
Async XLA Ops:
  2.7 10.9 %collective-permute-start.2 = (bf16[640,128]{1,0:T(8,128)(2,1)}, bf16[640,128]{1,0:T(8,128)(2,1)S(1)}, u32[]{:S(2)}, u32[]{:S(2)}) collective-permute-start(bf16[640,128]{1,0:T(8,128)(2,1)} %get-tuple-element.72.refs_0_), channel_id=1, source_target_pairs={{0,24},{8,16},{16,8},{24,0},{1,25},{9,17},{17,9},{25,1},{2,26},{10... | collective-permute-start | bytes 491528 | tf_op jit(solution)/shard_map/ppermute | solution.py:363
  7.8 14.1 %collective-permute-start.1 = (bf16[640,128]{1,0:T(8,128)(2,1)}, bf16[640,128]{1,0:T(8,128)(2,1)S(1)}, u32[]{:S(2)}, u32[]{:S(2)}) collective-permute-start(bf16[640,128]{1,0:T(8,128)(2,1)} %get-tuple-element.72.refs_0_), channel_id=1, source_target_pairs={{0,16},{8,24},{16,0},{24,8},{1,17},{9,25},{17,1},{25,9},{2,18},{10... | collective-permute-start | bytes 491528 | tf_op jit(solution)/shard_map/ppermute | solution.py:363
  7.8 14.1 %collective-permute-start = (bf16[640,128]{1,0:T(8,128)(2,1)}, bf16[640,128]{1,0:T(8,128)(2,1)S(1)}, u32[]{:S(2)}, u32[]{:S(2)}) collective-permute-start(bf16[640,128]{1,0:T(8,128)(2,1)} %get-tuple-element.72.refs_0_), channel_id=1, source_target_pairs={{0,8},{8,0},{16,24},{24,16},{1,9},{9,1},{17,25},{25,17},{2,10},{10... | collective-permute-start | bytes 491528 | tf_op jit(solution)/shard_map/ppermute | solution.py:363
  9.2 1.1 %copy-start = (bf16[1,192,16,128]{3,2,1,0:T(8,128)(2,1)S(1)}, bf16[1,192,16,128]{3,2,1,0:T(8,128)(2,1)}, u32[]{:S(2)}) copy-start(bf16[1,192,16,128]{3,2,1,0:T(8,128)(2,1)} %param.7) | copy-start | bytes 2359300
  10.3 1.1 %copy-start.1 = (bf16[1,192,16,128]{3,2,1,0:T(8,128)(2,1)S(1)}, bf16[1,192,16,128]{3,2,1,0:T(8,128)(2,1)}, u32[]{:S(2)}) copy-start(bf16[1,192,16,128]{3,2,1,0:T(8,128)(2,1)} %param.12) | copy-start | bytes 2359300
  11.4 0.9 %copy-start.2 = (bf16[640,128]{1,0:T(8,128)(2,1)S(1)}, bf16[640,128]{1,0:T(8,128)(2,1)}, u32[]{:S(2)}) copy-start(bf16[640,128]{1,0:T(8,128)(2,1)} %get-tuple-element.72.refs_0_) | copy-start | bytes 491524
  21.9 7.4 %collective-permute-start.3 = (bf16[1024,128]{1,0:T(8,128)(2,1)S(1)}, bf16[1024,128]{1,0:T(8,128)(2,1)S(1)}, u32[]{:S(2)}, u32[]{:S(2)}) collective-permute-start(bf16[1024,128]{1,0:T(8,128)(2,1)S(1)} %pad_maximum_fusion.refs_3_), channel_id=1, source_target_pairs={{0,4},{4,0},{1,5},{5,1},{2,6},{6,2},{3,7},{7,3},{8,12},{12,8},{9,1... | collective-permute-start | bytes 786440 | tf_op jit(solution)/shard_map/ppermute | solution.py:385
  23.5 14.8 %collective-permute-start.6 = (bf16[640,128]{1,0:T(8,128)(2,1)}, bf16[640,128]{1,0:T(8,128)(2,1)S(1)}, u32[]{:S(2)}, u32[]{:S(2)}) collective-permute-start(bf16[640,128]{1,0:T(8,128)(2,1)} %get-tuple-element.83.refs_1_), channel_id=1, source_target_pairs={{0,24},{8,16},{16,8},{24,0},{1,25},{9,17},{17,9},{25,1},{2,26},{10... | collective-permute-start | bytes 491528 | tf_op jit(solution)/shard_map/ppermute | solution.py:363
  26.0 12.8 %collective-permute-start.5 = (bf16[640,128]{1,0:T(8,128)(2,1)}, bf16[640,128]{1,0:T(8,128)(2,1)S(1)}, u32[]{:S(2)}, u32[]{:S(2)}) collective-permute-start(bf16[640,128]{1,0:T(8,128)(2,1)} %get-tuple-element.83.refs_1_), channel_id=1, source_target_pairs={{0,16},{8,24},{16,0},{24,8},{1,17},{9,25},{17,1},{25,9},{2,18},{10... | collective-permute-start | bytes 491528 | tf_op jit(solution)/shard_map/ppermute | solution.py:363
  26.0 12.8 %collective-permute-start.4 = (bf16[640,128]{1,0:T(8,128)(2,1)}, bf16[640,128]{1,0:T(8,128)(2,1)S(1)}, u32[]{:S(2)}, u32[]{:S(2)}) collective-permute-start(bf16[640,128]{1,0:T(8,128)(2,1)} %get-tuple-element.83.refs_1_), channel_id=1, source_target_pairs={{0,8},{8,0},{16,24},{24,16},{1,9},{9,1},{17,25},{25,17},{2,10},{10... | collective-permute-start | bytes 491528 | tf_op jit(solution)/shard_map/ppermute | solution.py:363
  38.8 7.3 %collective-permute-start.7 = (bf16[1024,128]{1,0:T(8,128)(2,1)S(1)}, bf16[1024,128]{1,0:T(8,128)(2,1)S(1)}, u32[]{:S(2)}, u32[]{:S(2)}) collective-permute-start(bf16[1024,128]{1,0:T(8,128)(2,1)S(1)} %pad_maximum_fusion.1.refs_3_), channel_id=1, source_target_pairs={{0,4},{4,0},{1,5},{5,1},{2,6},{6,2},{3,7},{7,3},{8,12},{12,8},{9,1... | collective-permute-start | bytes 786440 | tf_op jit(solution)/shard_map/ppermute | solution.py:385
  39.9 8.4 %collective-permute-start.8 = (bf16[768,128]{1,0:T(8,128)(2,1)S(1)}, bf16[768,128]{1,0:T(8,128)(2,1)S(1)}, u32[]{:S(2)}, u32[]{:S(2)}) collective-permute-start(bf16[768,128]{1,0:T(8,128)(2,1)S(1)} %get-tuple-element.100), channel_id=1, source_target_pairs={{8,0},{24,16},{16,24},{9,1},{25,17},{17,25},{10,2},{26,18},{18,26}... | collective-permute-start | bytes 589832 | tf_op jit(solution)/shard_map/ppermute | solution.py:363
  48.4 8.1 %collective-permute-start.9 = (bf16[384,128]{1,0:T(8,128)(2,1)S(1)}, bf16[384,128]{1,0:T(8,128)(2,1)S(1)}, u32[]{:S(2)}, u32[]{:S(2)}) collective-permute-start(bf16[384,128]{1,0:T(8,128)(2,1)S(1)} %get-tuple-element.102), channel_id=1, source_target_pairs={{16,0},{24,8},{17,1},{25,9},{18,2},{26,10},{19,3},{27,11},{20,4},{... | collective-permute-start | bytes 294920 | tf_op jit(solution)/shard_map/ppermute | solution.py:363
  49.9 6.7 %collective-permute-start.10 = (bf16[1024,128]{1,0:T(8,128)(2,1)S(1)}, bf16[1024,128]{1,0:T(8,128)(2,1)S(1)}, u32[]{:S(2)}, u32[]{:S(2)}) collective-permute-start(bf16[1024,128]{1,0:T(8,128)(2,1)S(1)} %get-tuple-element.104), channel_id=1, source_target_pairs={{0,4},{4,0},{1,5},{5,1},{2,6},{6,2},{3,7},{7,3},{8,12},{12,8},{9,1... | collective-permute-start | bytes 786440 | tf_op jit(solution)/shard_map/ppermute | solution.py:385
  58.8 6.4 %collective-permute-start.13 = (bf16[1024,128]{1,0:T(8,128)(2,1)S(1)}, bf16[1024,128]{1,0:T(8,128)(2,1)S(1)}, u32[]{:S(2)}, u32[]{:S(2)}) collective-permute-start(bf16[1024,128]{1,0:T(8,128)(2,1)S(1)} %get-tuple-element.128), channel_id=1, source_target_pairs={{0,4},{4,0},{1,5},{5,1},{2,6},{6,2},{3,7},{7,3},{8,12},{12,8},{9,1... | collective-permute-start | bytes 786440 | tf_op jit(solution)/shard_map/ppermute | solution.py:385
  60.4 9.0 %collective-permute-start.11 = (bf16[768,128]{1,0:T(8,128)(2,1)S(1)}, bf16[768,128]{1,0:T(8,128)(2,1)S(1)}, u32[]{:S(2)}, u32[]{:S(2)}) collective-permute-start(bf16[768,128]{1,0:T(8,128)(2,1)S(1)} %get-tuple-element.119), channel_id=1, source_target_pairs={{8,0},{24,16},{16,24},{9,1},{25,17},{17,25},{10,2},{26,18},{18,26}... | collective-permute-start | bytes 589832 | tf_op jit(solution)/shard_map/ppermute | solution.py:363
  61.7 10.1 %collective-permute-start.14 = (bf16[512,128]{1,0:T(8,128)(2,1)S(1)}, bf16[512,128]{1,0:T(8,128)(2,1)S(1)}, u32[]{:S(2)}, u32[]{:S(2)}) collective-permute-start(bf16[512,128]{1,0:T(8,128)(2,1)S(1)} %get-tuple-element.132), channel_id=1, source_target_pairs={{8,0},{0,8},{24,16},{16,24},{9,1},{1,9},{25,17},{17,25},{10,2},{2,... | collective-permute-start | bytes 393224 | tf_op jit(solution)/shard_map/ppermute | solution.py:363
  65.3 8.5 %collective-permute-start.15 = (bf16[512,128]{1,0:T(8,128)(2,1)S(1)}, bf16[512,128]{1,0:T(8,128)(2,1)S(1)}, u32[]{:S(2)}, u32[]{:S(2)}) collective-permute-start(bf16[512,128]{1,0:T(8,128)(2,1)S(1)} %get-tuple-element.133), channel_id=1, source_target_pairs={{8,0},{0,8},{24,16},{16,24},{9,1},{1,9},{25,17},{17,25},{10,2},{2,... | collective-permute-start | bytes 393224 | tf_op jit(solution)/shard_map/ppermute | solution.py:363
  69.5 12.8 %collective-permute-start.12 = (bf16[384,128]{1,0:T(8,128)(2,1)S(1)}, bf16[384,128]{1,0:T(8,128)(2,1)S(1)}, u32[]{:S(2)}, u32[]{:S(2)}) collective-permute-start(bf16[384,128]{1,0:T(8,128)(2,1)S(1)} %get-tuple-element.121), channel_id=1, source_target_pairs={{16,0},{24,8},{17,1},{25,9},{18,2},{26,10},{19,3},{27,11},{20,4},{... | collective-permute-start | bytes 294920 | tf_op jit(solution)/shard_map/ppermute | solution.py:363
  73.8 9.5 %collective-permute-start.16 = (bf16[512,128]{1,0:T(8,128)(2,1)S(1)}, bf16[512,128]{1,0:T(8,128)(2,1)S(1)}, u32[]{:S(2)}, u32[]{:S(2)}) collective-permute-start(bf16[512,128]{1,0:T(8,128)(2,1)S(1)} %get-tuple-element.135), channel_id=1, source_target_pairs={{0,16},{8,24},{16,0},{24,8},{1,17},{9,25},{17,1},{25,9},{2,18},{10... | collective-permute-start | bytes 393224 | tf_op jit(solution)/shard_map/ppermute | solution.py:363

commit v3 on v1

--- a/solution.py
+++ b/solution.py
@@ -364,7 +364,7 @@
     lines = send_over_roll(messages)
     block = math.gcd(flat, 256)
     steps = flat // block
-    heads, all_keys, line_own, line_got, roll_own, roll_got = [], [], [], [], [], []
+    heads, all_keys, line_own, line_got, roll_own, roll_got, near = [], [], [], [], [], [], []
     for g in range(groups):
         prompts = [(item, slot * prows, prows) for item in lines for slot in range(seq_size)]
         rollouts = [(item, prows, rrows) for item in messages]
@@ -390,8 +390,11 @@
             lines = send_over_roll(messages)
             roll_grads = [after(item, lines[0]) for item in roll_grads]
         roll_own.append(roll_grads[0])
-        roll_got.append([give_down(roll_grads[slot], slot) for slot in slots])
-
+        near.append(roll_grads[1])
+        roll_got.append([give_down(roll_grads[slot], slot) for slot in slots if slot > 1])
+
+    came = give_down(jnp.concatenate(near, axis=0), 1)
+    roll_got = [got + [came[g * rrows : (g + 1) * rrows]] for g, got in enumerate(roll_got)]
     sums = pair_sum(line_own, line_got, seq_size)
     attention_rows, grad_rows = row_outputs(heads, all_keys, row_count, block)
     grad_rk, grad_rv = finish(roll_own, roll_got, groups)

time: 84.3 us -> 82.9 us (0.983)
  starting transfers between devices: 29 us -> 27.1 us
    ppermute x4, waiting for transfers between devices: 4.48 us -> 7.91 us  [over_roll(): lax.ppermute(value, 'roll', [(i, (i + shift) % roll_size) for i in range(...]
    ppermute x15 -> x14, waiting for transfers between devices: 17.4 us -> 14.6 us  [over_seq(): return lax.ppermute(value, 'seq', which)]
    ppermute x4, starting transfers between devices: 5.26 us -> 3.81 us  [over_roll(): lax.ppermute(value, 'roll', [(i, (i + shift) % roll_size) for i in range(...]
    ppermute x15 -> x14, starting transfers between devices: 23.8 us -> 23.3 us  [over_seq(): return lax.ppermute(value, 'seq', which)]
  transfers between devices with their start and end apart: 19 -> 18, of which waited for: 8 -> 7; matrix products, arithmetic and copies ran while one was open for 0% -> 0% of each run, Pallas kernels for 30% -> 31%
where the time goes in v3:
time: 82.9 us; the launch traced here: 82.5 us
  Pallas kernels  28.1 us (34%)
  starting transfers between devices  27.1 us (33%)
  waiting for transfers between devices  22.5 us (27%)
  local copies, waits for them, and re-layouts  3.33 us (4%)
  between operations  1.5 us (2%)
    ppermute x14, starting transfers between devices, over_seq(): return lax.ppermute(value, 'seq', which)  23.3 us
    pallas_call x3, Pallas kernels, attend(): pl.pallas_call(body, out_shape=[jax.ShapeDtypeStruct(shape, kind) for sha...  18.5 us
    ppermute x14, waiting for transfers between devices, over_seq(): return lax.ppermute(value, 'seq', which)  14.6 us
    ppermute x4, waiting for transfers between devices, over_roll(): lax.ppermute(value, 'roll', [(i, (i + shift) % roll_size) for i in range(...  7.91 us
    pallas_call x1, Pallas kernels, row_outputs(): pl.pallas_call(body, out_shape=[jax.ShapeDtypeStruct((rows, per * groups,...  4.3 us
    ppermute x4, starting transfers between devices, over_roll(): lax.ppermute(value, 'roll', [(i, (i + shift) % roll_size) for i in range(...  3.81 us
    unnamed x6, local copies, waits for them, and re-layouts  3.18 us
    pallas_call x1, Pallas kernels, split_heads(): pl.pallas_call(body, out_shape=[jax.ShapeDtypeStruct((starts[-1], dim), B...  2.03 us
  transfers between devices with their start and end apart: 18, of which 7 were waited for; matrix products, arithmetic and copies ran while one was open for 0% of the time, Pallas kernels for 31%

profile of v3, /device:TPU:0, one launch (start us, length us, event | category | flops | bytes accessed | tf_op | source)
XLA Modules:
  0.0 82.5 jit_solution(7482160480869980740)
XLA Ops:
  0.6 2.0 %shard_map.118 = (bf16[640,128]{1,0:T(8,128)(2,1)}, bf16[640,128]{1,0:T(8,128)(2,1)}) custom-call(bf16[128,2,128]{2,1,0:T(2,128)(2,1)} %refs_0_.1, bf16[128,2,128]{2,1,0:T(2,128)(2,1)} %refs_1_.1, bf16[192,2,128]{2,1,0:T(2,128)(2,1)} %bitcast.17, bf16[192,2,128]{2,1,0:T(2,128)(2,1)} %bitcast.18), custom_call_target="tpu_custom_call" | custom-call | bytes 1310720 | tf_op jit(solution)/shard_map/pallas_call | solution.py:57
  2.7 5.1 %collective-permute-start.2 = (bf16[640,128]{1,0:T(8,128)(2,1)}, bf16[640,128]{1,0:T(8,128)(2,1)S(1)}, u32[]{:S(2)}, u32[]{:S(2)}) collective-permute-start(bf16[640,128]{1,0:T(8,128)(2,1)} %get-tuple-element.60.refs_0_), channel_id=1, source_target_pairs={{0,24},{8,16},{16,8},{24,0},{1,25},{9,17},{17,9},{25,1},{2,26},{10... | collective-permute-start | bytes 491528 | tf_op jit(solution)/shard_map/ppermute | solution.py:341
  7.8 0.0 collective-permute-start.1
  7.8 0.6 collective-permute-start
  9.1 0.1 stack.23.scalar_ref.refs_0_
  9.2 1.1 %copy-done = bf16[1,192,16,128]{3,2,1,0:T(8,128)(2,1)S(1)} copy-done((bf16[1,192,16,128]{3,2,1,0:T(8,128)(2,1)S(1)}, bf16[1,192,16,128]{3,2,1,0:T(8,128)(2,1)}, u32[]{:S(2)}) %copy-start) | copy-done | bytes 786456
  10.3 1.1 %copy-done.1 = bf16[1,192,16,128]{3,2,1,0:T(8,128)(2,1)S(1)} copy-done((bf16[1,192,16,128]{3,2,1,0:T(8,128)(2,1)S(1)}, bf16[1,192,16,128]{3,2,1,0:T(8,128)(2,1)}, u32[]{:S(2)}) %copy-start.1) | copy-done | bytes 786456
  11.4 0.9 %copy-done.2 = bf16[640,128]{1,0:T(8,128)(2,1)S(1)} copy-done((bf16[640,128]{1,0:T(8,128)(2,1)S(1)}, bf16[640,128]{1,0:T(8,128)(2,1)}, u32[]{:S(2)}) %copy-start.2) | copy-done | bytes 163864
  12.3 1.2 %shard_map.119 = (bf16[1536,128]{1,0:T(8,128)(2,1)S(1)}, bf16[1536,128]{1,0:T(8,128)(2,1)S(1)}, bf16[1536,128]{1,0:T(8,128)(2,1)S(1)}, bf16[1536,128]{1,0:T(8,12...) custom-call(s32[5]{0:T(128)S(1)} %stack.23.scalar_ref.refs_0_, ...), custom_call_target="tpu_custom_call" | custom-call | bytes 6291456 | tf_op jit(solution)/shard_map/pallas_call | solution.py:87
  13.6 0.0 collective-permute-done.2.refs_8_
  13.6 8.2 %collective-permute-done.1.refs_7_ = bf16[640,128]{1,0:T(8,128)(2,1)S(1)} collective-permute-done((bf16[640,128]{1,0:T(8,128)(2,1)}, bf16[640,128]{1,0:T(8,128)(2,1)S(1)}, u32[]{:S(2)}, u32[]{:S(2)}) %collective-permute-start.1) | collective-permute-done | bytes 163872 | tf_op jit(solution)/shard_map/ppermute | solution.py:341
  21.9 0.0 collective-permute-done.refs_6_
  21.9 1.6 %collective-permute-start.3 = (bf16[1024,128]{1,0:T(8,128)(2,1)S(1)}, bf16[1024,128]{1,0:T(8,128)(2,1)S(1)}, u32[]{:S(2)}, u32[]{:S(2)}) collective-permute-start(bf16[1024,128]{1,0:T(8,128)(2,1)S(1)} %pad_maximum_fusion.refs_3_), channel_id=1, source_target_pairs={{0,4},{4,0},{1,5},{5,1},{2,6},{6,2},{3,7},{7,3},{8,12},{12,8},{9,1... | collective-permute-start | bytes 786440 | tf_op jit(solution)/shard_map/ppermute | solution.py:350
  23.5 2.5 %collective-permute-start.6 = (bf16[640,128]{1,0:T(8,128)(2,1)}, bf16[640,128]{1,0:T(8,128)(2,1)S(1)}, u32[]{:S(2)}, u32[]{:S(2)}) collective-permute-start(bf16[640,128]{1,0:T(8,128)(2,1)} %get-tuple-element.71.refs_1_), channel_id=1, source_target_pairs={{0,24},{8,16},{16,8},{24,0},{1,25},{9,17},{17,9},{25,1},{2,26},{10... | collective-permute-start | bytes 491528 | tf_op jit(solution)/shard_map/ppermute | solution.py:341
  26.0 0.0 collective-permute-start.5
  26.0 1.9 %collective-permute-start.4 = (bf16[640,128]{1,0:T(8,128)(2,1)}, bf16[640,128]{1,0:T(8,128)(2,1)S(1)}, u32[]{:S(2)}, u32[]{:S(2)}) collective-permute-start(bf16[640,128]{1,0:T(8,128)(2,1)} %get-tuple-element.71.refs_1_), channel_id=1, source_target_pairs={{0,8},{8,0},{16,24},{24,16},{1,9},{9,1},{17,25},{25,17},{2,10},{10... | collective-permute-start | bytes 491528 | tf_op jit(solution)/shard_map/ppermute | solution.py:341
  27.9 1.5 %collective-permute-done.3.refs_4_ = bf16[1024,128]{1,0:T(8,128)(2,1)S(1)} collective-permute-done((bf16[1024,128]{1,0:T(8,128)(2,1)S(1)}, bf16[1024,128]{1,0:T(8,128)(2,1)S(1)}, u32[]{:S(2)}, u32[]{:S(2)}) %collective-permute-start.3) | collective-permute-done | bytes 262176 | tf_op jit(solution)/shard_map/ppermute | solution.py:350
  29.4 8.9 %shard_map.120 = (bf16[1536,128]{1,0:T(8,128)(2,1)S(1)}, bf16[1536,1792]{1,0:T(8,128)(2,1)S(1)}, bf16[1792,128]{1,0:T(8,128)(2,1)S(1)}, bf16[1792,128]{1,0:T(8,1...) custom-call(s32[5]{0:T(128)S(1)} %stack.23.scalar_ref.refs_0_, ...), custom_call_target="tpu_custom_call" | custom-call | flops 7046430720 | bytes 3145728 | tf_op jit(solution)/shard_map/pallas_call | solution.py:214
  38.2 0.0 collective-permute-done.6.refs_8_
  38.2 0.5 collective-permute-done.5.refs_7_
  38.7 0.0 collective-permute-done.4.refs_6_
  38.8 1.1 %collective-permute-start.7 = (bf16[1024,128]{1,0:T(8,128)(2,1)S(1)}, bf16[1024,128]{1,0:T(8,128)(2,1)S(1)}, u32[]{:S(2)}, u32[]{:S(2)}) collective-permute-start(bf16[1024,128]{1,0:T(8,128)(2,1)S(1)} %pad_maximum_fusion.1.refs_3_), channel_id=1, source_target_pairs={{0,4},{4,0},{1,5},{5,1},{2,6},{6,2},{3,7},{7,3},{8,12},{12,8},{9,1... | collective-permute-start | bytes 786440 | tf_op jit(solution)/shard_map/ppermute | solution.py:350
  39.9 1.3 %collective-permute-start.8 = (bf16[384,128]{1,0:T(8,128)(2,1)S(1)}, bf16[384,128]{1,0:T(8,128)(2,1)S(1)}, u32[]{:S(2)}, u32[]{:S(2)}) collective-permute-start(bf16[384,128]{1,0:T(8,128)(2,1)S(1)} %get-tuple-element.79), channel_id=1, source_target_pairs={{16,0},{24,8},{17,1},{25,9},{18,2},{26,10},{19,3},{27,11},{20,4},{... | collective-permute-start | bytes 294920 | tf_op jit(solution)/shard_map/ppermute | solution.py:341
  41.2 1.5 %collective-permute-start.9 = (bf16[384,128]{1,0:T(8,128)(2,1)S(1)}, bf16[384,128]{1,0:T(8,128)(2,1)S(1)}, u32[]{:S(2)}, u32[]{:S(2)}) collective-permute-start(bf16[384,128]{1,0:T(8,128)(2,1)S(1)} %get-tuple-element.81), channel_id=1, source_target_pairs={{24,0},{16,8},{25,1},{17,9},{26,2},{18,10},{27,3},{19,11},{28,4},{... | collective-permute-start | bytes 294920 | tf_op jit(solution)/shard_map/ppermute | solution.py:341
  42.7 1.1 %collective-permute-start.13 = (bf16[1024,128]{1,0:T(8,128)(2,1)S(1)}, bf16[1024,128]{1,0:T(8,128)(2,1)S(1)}, u32[]{:S(2)}, u32[]{:S(2)}) collective-permute-start(bf16[1024,128]{1,0:T(8,128)(2,1)S(1)} %get-tuple-element.106), channel_id=1, source_target_pairs={{0,4},{4,0},{1,5},{5,1},{2,6},{6,2},{3,7},{7,3},{8,12},{12,8},{9,1... | collective-permute-start | bytes 786440 | tf_op jit(solution)/shard_map/ppermute | solution.py:350
  43.8 4.4 %collective-permute-done.7.refs_4_ = bf16[1024,128]{1,0:T(8,128)(2,1)S(1)} collective-permute-done((bf16[1024,128]{1,0:T(8,128)(2,1)S(1)}, bf16[1024,128]{1,0:T(8,128)(2,1)S(1)}, u32[]{:S(2)}, u32[]{:S(2)}) %collective-permute-start.7) | collective-permute-done | bytes 262176 | tf_op jit(solution)/shard_map/ppermute | solution.py:350
  48.1 4.8 %shard_map.121 = (bf16[768,128]{1,0:T(8,128)(2,1)S(1)}, bf16[768,1792]{1,0:T(8,128)(2,1)S(1)}, bf16[1792,128]{1,0:T(8,128)(2,1)S(1)}, bf16[1792,128]{1,0:T(8,128...) custom-call(s32[5]{0:T(128)S(1)} %stack.23.scalar_ref.refs_0_, ...), custom_call_target="tpu_custom_call" | custom-call | flops 3523215360 | bytes 1572864 | tf_op jit(solution)/shard_map/pallas_call | solution.py:214
  52.9 0.0 collective-permute-done.8.refs_2_
  52.9 0.0 collective-permute-done.9.refs_3_
  52.9 4.8 %shard_map.122 = (bf16[768,128]{1,0:T(8,128)(2,1)S(1)}, bf16[768,1792]{1,0:T(8,128)(2,1)S(1)}, f32[1024,128]{1,0:T(8,128)S(1)}, bf16[1024,128]{1,0:T(8,128)(2,1)...) custom-call(s32[5]{0:T(128)S(1)} %stack.23.scalar_ref.refs_0_, ...), custom_call_target="tpu_custom_call" | custom-call | flops 3523215360 | bytes 1572864 | tf_op jit(solution)/shard_map/pallas_call | solution.py:214
  57.8 1.3 %collective-permute-start.11 = (bf16[384,128]{1,0:T(8,128)(2,1)S(1)}, bf16[384,128]{1,0:T(8,128)(2,1)S(1)}, u32[]{:S(2)}, u32[]{:S(2)}) collective-permute-start(bf16[384,128]{1,0:T(8,128)(2,1)S(1)} %get-tuple-element.100), channel_id=1, source_target_pairs={{16,0},{24,8},{17,1},{25,9},{18,2},{26,10},{19,3},{27,11},{20,4},{... | collective-permute-start | bytes 294920 | tf_op jit(solution)/shard_map/ppermute | solution.py:341
  59.1 1.3 %collective-permute-start.12 = (bf16[384,128]{1,0:T(8,128)(2,1)S(1)}, bf16[384,128]{1,0:T(8,128)(2,1)S(1)}, u32[]{:S(2)}, u32[]{:S(2)}) collective-permute-start(bf16[384,128]{1,0:T(8,128)(2,1)S(1)} %get-tuple-element.101), channel_id=1, source_target_pairs={{24,0},{16,8},{25,1},{17,9},{26,2},{18,10},{27,3},{19,11},{28,4},{... | collective-permute-start | bytes 294920 | tf_op jit(solution)/shard_map/ppermute | solution.py:341
  60.4 1.5 %collective-permute-start.10 = (bf16[768,128]{1,0:T(8,128)(2,1)S(1)}, bf16[768,128]{1,0:T(8,128)(2,1)S(1)}, u32[]{:S(2)}, u32[]{:S(2)}) collective-permute-start(bf16[768,128]{1,0:T(8,128)(2,1)S(1)} %pad_maximum_fusion.2), channel_id=1, source_target_pairs={{8,0},{24,16},{9,1},{25,17},{10,2},{26,18},{11,3},{27,19},{12,4},{... | collective-permute-start | bytes 589832 | tf_op jit(solution)/shard_map/ppermute | solution.py:341
  61.9 0.1 collective-permute-start.14
  62.0 4.3 %shard_map.123 = (bf16[192,16,128]{2,1,0:T(8,128)(2,1)}, bf16[192,16,128]{2,1,0:T(8,128)(2,1)}) custom-call(bf16[1536,128]{1,0:T(8,128)(2,1)S(1)} %get-tuple-element.65.refs_0_, bf16[1536,1792]{1,0:T(8,128)(2,1)S(1)} %get-tuple-element.66.refs_1_, bf16[768,128]{1,0:T(8,128)(2,1)S(1)} %get-tuple-element.75.refs_2_, ...), custom_call_target="tpu_custom_call" | custom-call | flops 2818572288 | bytes 11010048 | tf_op jit(solution)/shard_map/pallas_call | solution.py:257
  66.3 0.0 collective-permute-done.13.refs_2_
  66.3 2.0 %collective-permute-done.14.refs_3_ = bf16[1024,128]{1,0:T(8,128)(2,1)S(1)} collective-permute-done((bf16[1024,128]{1,0:T(8,128)(2,1)S(1)}, bf16[1024,128]{1,0:T(8,128)(2,1)S(1)}, u32[]{:S(2)}, u32[]{:S(2)}) %collective-permute-start.14) | collective-permute-done | bytes 262176 | tf_op jit(solution)/shard_map/ppermute | solution.py:350
  68.4 0.1 shard_map.125
  68.5 2.7 %collective-permute-start.15 = (bf16[512,128]{1,0:T(8,128)(2,1)S(1)}, bf16[512,128]{1,0:T(8,128)(2,1)S(1)}, u32[]{:S(2)}, u32[]{:S(2)}) collective-permute-start(bf16[512,128]{1,0:T(8,128)(2,1)S(1)} %get-tuple-element.109), channel_id=1, source_target_pairs={{8,0},{0,8},{24,16},{16,24},{9,1},{1,9},{25,17},{17,25},{10,2},{2,... | collective-permute-start | bytes 393224 | tf_op jit(solution)/shard_map/ppermute | solution.py:341
  71.2 3.5 %collective-permute-start.16 = (bf16[512,128]{1,0:T(8,128)(2,1)S(1)}, bf16[512,128]{1,0:T(8,128)(2,1)S(1)}, u32[]{:S(2)}, u32[]{:S(2)}) collective-permute-start(bf16[512,128]{1,0:T(8,128)(2,1)S(1)} %get-tuple-element.110), channel_id=1, source_target_pairs={{16,0},{24,8},{0,16},{8,24},{17,1},{25,9},{1,17},{9,25},{18,2},{26... | collective-permute-start | bytes 393224 | tf_op jit(solution)/shard_map/ppermute | solution.py:341
  74.7 0.0 collective-permute-done.10
  74.7 0.0 collective-permute-start.17
  74.8 0.0 collective-permute-done.11.refs_5_
  74.8 1.0 %shard_map.124 = (bf16[192,2,128]{2,1,0:T(2,128)(2,1)}, bf16[192,2,128]{2,1,0:T(2,128)(2,1)}) custom-call(f32[384,128]{1,0:T(8,128)S(1)} %get-tuple-element.95.refs_0_, f32[384,128]{1,0:T(8,128)S(1)} %get-tuple-element.96.refs_1_, bf16[384,128]{1,0:T(8,128)(2,1)S(1)} %collective-permute-done.8.refs_2_, bf16[384,128]{1,0:T(8,128)(2,1)S(1)} %collective-permute-done.9.refs_3_, ...), custom_call_target="tpu_custom_call" | custom-call | flops 294912 | bytes 983040 | tf_op jit(solution)/shard_map/pallas_call | solution.py:313
  75.8 0.0 collective-permute-done.15.refs_1_
  75.8 3.3 %collective-permute-done.16.refs_2_ = bf16[512,128]{1,0:T(8,128)(2,1)S(1)} collective-permute-done((bf16[512,128]{1,0:T(8,128)(2,1)S(1)}, bf16[512,128]{1,0:T(8,128)(2,1)S(1)}, u32[]{:S(2)}, u32[]{:S(2)}) %collective-permute-start.16) | collective-permute-done | bytes 131104 | tf_op jit(solution)/shard_map/ppermute | solution.py:341
  79.1 2.5 %collective-permute-done.17.refs_3_ = bf16[512,128]{1,0:T(8,128)(2,1)S(1)} collective-permute-done((bf16[512,128]{1,0:T(8,128)(2,1)S(1)}, bf16[512,128]{1,0:T(8,128)(2,1)S(1)}, u32[]{:S(2)}, u32[]{:S(2)}) %collective-permute-start.17) | collective-permute-done | bytes 131104 | tf_op jit(solution)/shard_map/ppermute | solution.py:341
  81.6 0.9 %shard_map.126 = (bf16[128,2,128]{2,1,0:T(2,128)(2,1)}, bf16[128,2,128]{2,1,0:T(2,128)(2,1)}) custom-call(f32[512,128]{1,0:T(8,128)S(1)} %get-tuple-element.108.refs_0_, bf16[512,128]{1,0:T(8,128)(2,1)S(1)} %collective-permute-done.15.refs_1_, bf16[512,128]{1,0:T(8,128)(2,1)S(1)} %collective-permute-done.16.refs_2_, ...), custom_call_target="tpu_custom_call" | custom-call | flops 196608 | bytes 655360 | tf_op jit(solution)/shard_map/pallas_call | solution.py:313
  (16 shorter events, 0.1 us)
Async XLA Ops:
  2.7 10.9 %collective-permute-start.2 = (bf16[640,128]{1,0:T(8,128)(2,1)}, bf16[640,128]{1,0:T(8,128)(2,1)S(1)}, u32[]{:S(2)}, u32[]{:S(2)}) collective-permute-start(bf16[640,128]{1,0:T(8,128)(2,1)} %get-tuple-element.60.refs_0_), channel_id=1, source_target_pairs={{0,24},{8,16},{16,8},{24,0},{1,25},{9,17},{17,9},{25,1},{2,26},{10... | collective-permute-start | bytes 491528 | tf_op jit(solution)/shard_map/ppermute | solution.py:341
  7.8 14.1 %collective-permute-start.1 = (bf16[640,128]{1,0:T(8,128)(2,1)}, bf16[640,128]{1,0:T(8,128)(2,1)S(1)}, u32[]{:S(2)}, u32[]{:S(2)}) collective-permute-start(bf16[640,128]{1,0:T(8,128)(2,1)} %get-tuple-element.60.refs_0_), channel_id=1, source_target_pairs={{0,16},{8,24},{16,0},{24,8},{1,17},{9,25},{17,1},{25,9},{2,18},{10... | collective-permute-start | bytes 491528 | tf_op jit(solution)/shard_map/ppermute | solution.py:341
  7.8 14.1 %collective-permute-start = (bf16[640,128]{1,0:T(8,128)(2,1)}, bf16[640,128]{1,0:T(8,128)(2,1)S(1)}, u32[]{:S(2)}, u32[]{:S(2)}) collective-permute-start(bf16[640,128]{1,0:T(8,128)(2,1)} %get-tuple-element.60.refs_0_), channel_id=1, source_target_pairs={{0,8},{8,0},{16,24},{24,16},{1,9},{9,1},{17,25},{25,17},{2,10},{10... | collective-permute-start | bytes 491528 | tf_op jit(solution)/shard_map/ppermute | solution.py:341
  9.2 1.1 %copy-start = (bf16[1,192,16,128]{3,2,1,0:T(8,128)(2,1)S(1)}, bf16[1,192,16,128]{3,2,1,0:T(8,128)(2,1)}, u32[]{:S(2)}) copy-start(bf16[1,192,16,128]{3,2,1,0:T(8,128)(2,1)} %param.7) | copy-start | bytes 2359300
  10.3 1.1 %copy-start.1 = (bf16[1,192,16,128]{3,2,1,0:T(8,128)(2,1)S(1)}, bf16[1,192,16,128]{3,2,1,0:T(8,128)(2,1)}, u32[]{:S(2)}) copy-start(bf16[1,192,16,128]{3,2,1,0:T(8,128)(2,1)} %param.12) | copy-start | bytes 2359300
  11.4 0.9 %copy-start.2 = (bf16[640,128]{1,0:T(8,128)(2,1)S(1)}, bf16[640,128]{1,0:T(8,128)(2,1)}, u32[]{:S(2)}) copy-start(bf16[640,128]{1,0:T(8,128)(2,1)} %get-tuple-element.60.refs_0_) | copy-start | bytes 491524
  21.9 7.4 %collective-permute-start.3 = (bf16[1024,128]{1,0:T(8,128)(2,1)S(1)}, bf16[1024,128]{1,0:T(8,128)(2,1)S(1)}, u32[]{:S(2)}, u32[]{:S(2)}) collective-permute-start(bf16[1024,128]{1,0:T(8,128)(2,1)S(1)} %pad_maximum_fusion.refs_3_), channel_id=1, source_target_pairs={{0,4},{4,0},{1,5},{5,1},{2,6},{6,2},{3,7},{7,3},{8,12},{12,8},{9,1... | collective-permute-start | bytes 786440 | tf_op jit(solution)/shard_map/ppermute | solution.py:350
  23.5 14.7 %collective-permute-start.6 = (bf16[640,128]{1,0:T(8,128)(2,1)}, bf16[640,128]{1,0:T(8,128)(2,1)S(1)}, u32[]{:S(2)}, u32[]{:S(2)}) collective-permute-start(bf16[640,128]{1,0:T(8,128)(2,1)} %get-tuple-element.71.refs_1_), channel_id=1, source_target_pairs={{0,24},{8,16},{16,8},{24,0},{1,25},{9,17},{17,9},{25,1},{2,26},{10... | collective-permute-start | bytes 491528 | tf_op jit(solution)/shard_map/ppermute | solution.py:341
  26.0 12.8 %collective-permute-start.5 = (bf16[640,128]{1,0:T(8,128)(2,1)}, bf16[640,128]{1,0:T(8,128)(2,1)S(1)}, u32[]{:S(2)}, u32[]{:S(2)}) collective-permute-start(bf16[640,128]{1,0:T(8,128)(2,1)} %get-tuple-element.71.refs_1_), channel_id=1, source_target_pairs={{0,16},{8,24},{16,0},{24,8},{1,17},{9,25},{17,1},{25,9},{2,18},{10... | collective-permute-start | bytes 491528 | tf_op jit(solution)/shard_map/ppermute | solution.py:341
  26.0 12.8 %collective-permute-start.4 = (bf16[640,128]{1,0:T(8,128)(2,1)}, bf16[640,128]{1,0:T(8,128)(2,1)S(1)}, u32[]{:S(2)}, u32[]{:S(2)}) collective-permute-start(bf16[640,128]{1,0:T(8,128)(2,1)} %get-tuple-element.71.refs_1_), channel_id=1, source_target_pairs={{0,8},{8,0},{16,24},{24,16},{1,9},{9,1},{17,25},{25,17},{2,10},{10... | collective-permute-start | bytes 491528 | tf_op jit(solution)/shard_map/ppermute | solution.py:341
  38.8 9.3 %collective-permute-start.7 = (bf16[1024,128]{1,0:T(8,128)(2,1)S(1)}, bf16[1024,128]{1,0:T(8,128)(2,1)S(1)}, u32[]{:S(2)}, u32[]{:S(2)}) collective-permute-start(bf16[1024,128]{1,0:T(8,128)(2,1)S(1)} %pad_maximum_fusion.1.refs_3_), channel_id=1, source_target_pairs={{0,4},{4,0},{1,5},{5,1},{2,6},{6,2},{3,7},{7,3},{8,12},{12,8},{9,1... | collective-permute-start | bytes 786440 | tf_op jit(solution)/shard_map/ppermute | solution.py:350
  39.9 13.0 %collective-permute-start.8 = (bf16[384,128]{1,0:T(8,128)(2,1)S(1)}, bf16[384,128]{1,0:T(8,128)(2,1)S(1)}, u32[]{:S(2)}, u32[]{:S(2)}) collective-permute-start(bf16[384,128]{1,0:T(8,128)(2,1)S(1)} %get-tuple-element.79), channel_id=1, source_target_pairs={{16,0},{24,8},{17,1},{25,9},{18,2},{26,10},{19,3},{27,11},{20,4},{... | collective-permute-start | bytes 294920 | tf_op jit(solution)/shard_map/ppermute | solution.py:341
  41.2 11.8 %collective-permute-start.9 = (bf16[384,128]{1,0:T(8,128)(2,1)S(1)}, bf16[384,128]{1,0:T(8,128)(2,1)S(1)}, u32[]{:S(2)}, u32[]{:S(2)}) collective-permute-start(bf16[384,128]{1,0:T(8,128)(2,1)S(1)} %get-tuple-element.81), channel_id=1, source_target_pairs={{24,0},{16,8},{25,1},{17,9},{26,2},{18,10},{27,3},{19,11},{28,4},{... | collective-permute-start | bytes 294920 | tf_op jit(solution)/shard_map/ppermute | solution.py:341
  42.7 23.7 %collective-permute-start.13 = (bf16[1024,128]{1,0:T(8,128)(2,1)S(1)}, bf16[1024,128]{1,0:T(8,128)(2,1)S(1)}, u32[]{:S(2)}, u32[]{:S(2)}) collective-permute-start(bf16[1024,128]{1,0:T(8,128)(2,1)S(1)} %get-tuple-element.106), channel_id=1, source_target_pairs={{0,4},{4,0},{1,5},{5,1},{2,6},{6,2},{3,7},{7,3},{8,12},{12,8},{9,1... | collective-permute-start | bytes 786440 | tf_op jit(solution)/shard_map/ppermute | solution.py:350
  57.8 17.0 %collective-permute-start.11 = (bf16[384,128]{1,0:T(8,128)(2,1)S(1)}, bf16[384,128]{1,0:T(8,128)(2,1)S(1)}, u32[]{:S(2)}, u32[]{:S(2)}) collective-permute-start(bf16[384,128]{1,0:T(8,128)(2,1)S(1)} %get-tuple-element.100), channel_id=1, source_target_pairs={{16,0},{24,8},{17,1},{25,9},{18,2},{26,10},{19,3},{27,11},{20,4},{... | collective-permute-start | bytes 294920 | tf_op jit(solution)/shard_map/ppermute | solution.py:341
  59.1 15.7 %collective-permute-start.12 = (bf16[384,128]{1,0:T(8,128)(2,1)S(1)}, bf16[384,128]{1,0:T(8,128)(2,1)S(1)}, u32[]{:S(2)}, u32[]{:S(2)}) collective-permute-start(bf16[384,128]{1,0:T(8,128)(2,1)S(1)} %get-tuple-element.101), channel_id=1, source_target_pairs={{24,0},{16,8},{25,1},{17,9},{26,2},{18,10},{27,3},{19,11},{28,4},{... | collective-permute-start | bytes 294920 | tf_op jit(solution)/shard_map/ppermute | solution.py:341
  60.4 14.3 %collective-permute-start.10 = (bf16[768,128]{1,0:T(8,128)(2,1)S(1)}, bf16[768,128]{1,0:T(8,128)(2,1)S(1)}, u32[]{:S(2)}, u32[]{:S(2)}) collective-permute-start(bf16[768,128]{1,0:T(8,128)(2,1)S(1)} %pad_maximum_fusion.2), channel_id=1, source_target_pairs={{8,0},{24,16},{9,1},{25,17},{10,2},{26,18},{11,3},{27,19},{12,4},{... | collective-permute-start | bytes 589832 | tf_op jit(solution)/shard_map/ppermute | solution.py:341
  61.9 6.4 %collective-permute-start.14 = (bf16[1024,128]{1,0:T(8,128)(2,1)S(1)}, bf16[1024,128]{1,0:T(8,128)(2,1)S(1)}, u32[]{:S(2)}, u32[]{:S(2)}) collective-permute-start(bf16[1024,128]{1,0:T(8,128)(2,1)S(1)} %get-tuple-element.107), channel_id=1, source_target_pairs={{0,4},{4,0},{1,5},{5,1},{2,6},{6,2},{3,7},{7,3},{8,12},{12,8},{9,1... | collective-permute-start | bytes 786440 | tf_op jit(solution)/shard_map/ppermute | solution.py:350
  68.5 7.4 %collective-permute-start.15 = (bf16[512,128]{1,0:T(8,128)(2,1)S(1)}, bf16[512,128]{1,0:T(8,128)(2,1)S(1)}, u32[]{:S(2)}, u32[]{:S(2)}) collective-permute-start(bf16[512,128]{1,0:T(8,128)(2,1)S(1)} %get-tuple-element.109), channel_id=1, source_target_pairs={{8,0},{0,8},{24,16},{16,24},{9,1},{1,9},{25,17},{17,25},{10,2},{2,... | collective-permute-start | bytes 393224 | tf_op jit(solution)/shard_map/ppermute | solution.py:341
  71.2 7.9 %collective-permute-start.16 = (bf16[512,128]{1,0:T(8,128)(2,1)S(1)}, bf16[512,128]{1,0:T(8,128)(2,1)S(1)}, u32[]{:S(2)}, u32[]{:S(2)}) collective-permute-start(bf16[512,128]{1,0:T(8,128)(2,1)S(1)} %get-tuple-element.110), channel_id=1, source_target_pairs={{16,0},{24,8},{0,16},{8,24},{17,1},{25,9},{1,17},{9,25},{18,2},{26... | collective-permute-start | bytes 393224 | tf_op jit(solution)/shard_map/ppermute | solution.py:341
  74.7 6.9 %collective-permute-start.17 = (bf16[512,128]{1,0:T(8,128)(2,1)S(1)}, bf16[512,128]{1,0:T(8,128)(2,1)S(1)}, u32[]{:S(2)}, u32[]{:S(2)}) collective-permute-start(bf16[512,128]{1,0:T(8,128)(2,1)S(1)} %get-tuple-element.111), channel_id=1, source_target_pairs={{24,0},{16,8},{8,16},{0,24},{25,1},{17,9},{9,17},{1,25},{26,2},{18... | collective-permute-start | bytes 393224 | tf_op jit(solution)/shard_map/ppermute | solution.py:341
